TPU v7x, 256 devices: a whole 4x4x8 slice. The times are simulated.
256 devices in a mesh: visit: 32 (over x, z), sky: 8 (over y, core).
Axes of the slice: x: 4, y: 4, z: 8, core: 2. Of those that a mesh axis runs over, the one named last changes fastest.
Arguments:
- ccd_tiles: bfloat16 [256, 64, 2048], P(('visit', 'sky')), may hold values from -6 to 6
- row_taps: bfloat16 [5, 41], replicated, may hold values from -1 to 1
- col_taps: bfloat16 [5, 41], replicated, may hold values from -1 to 1
- psf_coeffs: float32 [256, 5, 3], P(('visit', 'sky')), may hold values from -3 to 3
- warp_start_x: int32 [256, 2048], P(('visit', 'sky')), may hold values from 2 to 2044
- warp_frac_x: float32 [256, 2048], P(('visit', 'sky')), may hold values from 0.05 to 0.95
- warp_start_y: int32 [256, 64], P(('visit', 'sky')), may hold values from 2 to 60
- warp_frac_y: float32 [256, 64], P(('visit', 'sky')), may hold values from 0.05 to 0.95
- tile_weight: bfloat16 [256], P(('visit', 'sky')), may hold values from 0.25 to 4
- strip_owner: int32 [256, 16, 1], P(('visit', 'sky')), may hold values from 0 to 31; in each aligned block of 16 rows (0 to 15, 16 to 31, ..., all dimensions but the last counted through in order) at most 2 rows name the same one
- strip_block: int32 [256, 16], P(('visit', 'sky')), may hold values from 0 to 15
Outputs:
- coadd: float32 [512, 65536], P('sky', 'visit')
- detection: float32 [512, 65536], P('sky', 'visit')
Inputs may be any that keep to these rules, and one draw needn't show every extreme that they name: `strip_owner`: among the strips of one device (aligned blocks of 16 strips) no patch is named more than 2 times; some patch is named exactly 2 times in some device's strips.
All inputs are finite; a program needn't handle non-finite values.
Results may differ from a plain program's by a relative error of at most 0.0068.
Values may be sent and summed in bfloat16 or wider, within the bound.
No kernel may reach another device: no remote copies, remote signals or barrier semaphores. Data moves between devices by JAX's collectives and lax.ppermute only.
A program may use at most 128 MiB of HBM per device.

v0:
```python
import jax
import jax.numpy as jnp
from jax import lax
from jax.sharding import PartitionSpec as P

KW = 41
HALO = 20


def padded_2(value, sides, width):
    for axis, dim in sides:
        size, length = (lax.axis_size(axis), value.shape[dim])
        up = [(i, (i + 1) % size) for i in range(size - 1)]
        down = [(j, i) for i, j in up]
        last = lax.slice_in_dim(value, length - width, length, axis=dim)
        initial = lax.slice_in_dim(value, 0, width, axis=dim)
        before = lax.ppermute(last, axis, up)
        after = lax.ppermute(initial, axis, down)
        value = jnp.concatenate([before, value, after], axis=dim)
    return value


def lanczos(offset):
    return (
        3.0
        * jnp.sin(jnp.pi * offset)
        * jnp.sin(jnp.pi * offset / 3.0)
        / (jnp.pi * jnp.pi * offset * offset)
    )


def coefficient_maps(coefficients, num_rows, num_cols):
    x_coord = (2.0 * jnp.arange(num_cols, dtype=jnp.float32) - (num_cols - 1)) / (num_cols - 1)
    y_coord = (2.0 * jnp.arange(num_rows, dtype=jnp.float32) - (num_rows - 1)) / (num_rows - 1)
    return (
        coefficients[:, 0, None, None]
        + coefficients[:, 1, None, None] * x_coord[None, None, :]
        + coefficients[:, 2, None, None] * y_coord[None, :, None]
    )


def band_matrix(tap_values, length):
    indices = jnp.arange(length)
    offset = indices[None, :] - indices[:, None] + HALO
    inside = (offset >= 0) & (offset < KW)
    return jnp.where(
        inside, tap_values[jnp.clip(offset, 0, KW - 1)], jnp.zeros((), tap_values.dtype)
    )


def lanczos_matrix(starts, fractions, length):
    step_off = jnp.arange(length)[None, :] - starts[:, None]
    inside = (step_off >= -2) & (step_off <= 3)
    values = lanczos(fractions[:, None] - step_off.astype(jnp.float32))
    return jnp.where(inside, values, 0.0).astype(jnp.bfloat16)


def filter_rows(padded, smooth_taps, out_rows):
    result = jnp.zeros((out_rows, padded.shape[1]), jnp.float32)
    for offset in range(2 * HALO + 1):
        result = result + smooth_taps[offset] * padded[offset : offset + out_rows, :]
    return result


def filter_columns(padded, smooth_taps, out_cols):
    result = jnp.zeros((padded.shape[0], out_cols), jnp.float32)
    for offset in range(2 * HALO + 1):
        result = result + smooth_taps[offset] * padded[:, offset : offset + out_cols]
    return result


def contract_last(left, right, **unused):
    return lax.dot_general(
        left, right, (((1,), (1,)), ((), ())), preferred_element_type=jnp.float32
    )


def local(
    ccd_tiles,
    row_taps,
    col_taps,
    psf_coeffs,
    warp_start_x,
    warp_frac_x,
    warp_start_y,
    warp_frac_y,
    tile_weight,
    strip_owner,
    strip_block,
):
    tile_count, tile_rows, tile_cols = ccd_tiles.shape
    per_tile = tile_cols // 128
    peer_count = lax.axis_size("visit")
    num_strips = tile_count * per_tile
    basis_count = row_taps.shape[0]
    row_bands = [band_matrix(row_taps[basis_idx], tile_cols) for basis_idx in range(basis_count)]
    col_bands = [band_matrix(col_taps[basis_idx], tile_rows) for basis_idx in range(basis_count)]
    strip_list = []
    for tile_idx in range(tile_count):
        maps = coefficient_maps(psf_coeffs[tile_idx], tile_rows, tile_cols)
        matched = jnp.zeros((tile_rows, tile_cols), jnp.float32)
        for basis_idx in range(basis_count):
            across = contract_last(ccd_tiles[tile_idx], row_bands[basis_idx]).astype(jnp.bfloat16)
            basis_term = jnp.dot(col_bands[basis_idx], across, preferred_element_type=jnp.float32)
            matched = matched + maps[basis_idx] * basis_term
        matched = matched.astype(jnp.bfloat16)
        warp_cols = lanczos_matrix(warp_start_x[tile_idx], warp_frac_x[tile_idx], tile_cols)
        col_warped = contract_last(matched, warp_cols).astype(jnp.bfloat16)
        warp_rows = lanczos_matrix(warp_start_y[tile_idx], warp_frac_y[tile_idx], tile_rows)
        warped = jnp.dot(warp_rows, col_warped, preferred_element_type=jnp.float32).astype(
            jnp.bfloat16
        )
        strip_list.append(warped.reshape(tile_rows, per_tile, 128).transpose(1, 0, 2))
    pieces = jnp.concatenate(strip_list, 0)
    owner_flat = strip_owner.reshape(-1)
    block_flat = strip_block.reshape(-1)
    strip_weight = jnp.repeat(tile_weight, per_tile)
    canvas_col = owner_flat * per_tile + block_flat
    spread_w = (
        jnp.zeros((num_strips, peer_count * per_tile), jnp.bfloat16)
        .at[jnp.arange(num_strips), canvas_col]
        .set(strip_weight)
    )
    canvas = jnp.einsum("bc,brk->crk", spread_w, pieces, preferred_element_type=jnp.float32)
    canvas_w = jnp.sum(spread_w.astype(jnp.float32), 0)
    numerator, weight_sum = (
        lax.psum_scatter(
            canvas.reshape(peer_count, per_tile, tile_rows, 128),
            "visit",
            scatter_dimension=0,
            tiled=True,
        ),
        lax.psum_scatter(
            canvas_w.reshape(peer_count, per_tile), "visit", scatter_dimension=0, tiled=True
        ),
    )
    numerator = numerator[0]
    weight_sum = weight_sum[0]
    coadded = (
        (numerator / (weight_sum[:, None, None] + 1.0))
        .transpose(1, 0, 2)
        .reshape(tile_rows, tile_cols)
    )
    smooth_taps = 1.0 - (jnp.arange(-HALO, HALO + 1).astype(jnp.float32) / 21.0) ** 2
    noise_norm = jnp.sum(smooth_taps * smooth_taps)
    padded = padded_2(coadded, (("visit", 1), ("sky", 0)), HALO)
    vertical = filter_rows(padded, smooth_taps, tile_rows)
    smoothed = filter_columns(vertical, smooth_taps, tile_cols)
    return (coadded, smoothed / noise_norm)


def solution(mesh):
    in_specs = (
        P(("visit", "sky"), None, None),
        P(),
        P(),
        P(("visit", "sky"), None, None),
        P(("visit", "sky"), None),
        P(("visit", "sky"), None),
        P(("visit", "sky"), None),
        P(("visit", "sky"), None),
        P(("visit", "sky")),
        P(("visit", "sky"), None, None),
        P(("visit", "sky"), None),
    )
    out_specs = (P("sky", "visit"), P("sky", "visit"))
    return jax.shard_map(local, mesh=mesh, in_specs=in_specs, out_specs=out_specs, check_vma=False)
```

profile of v0, /device:TPU:1, one launch (start us, length us, event | category | flops | bytes accessed | tf_op | source)
XLA Modules:
  0.0 863.5 jit_solution(9623286528198044792)
XLA Ops:
  7.2 0.0 copy-start
  7.2 0.0 all-reduce.4.cloned.1.call-start
  7.2 2.1 fusion.1261
  9.3 2.1 fusion.1260
  11.4 2.1 fusion.1259
  13.6 2.1 fusion.1263
  15.7 2.1 fusion.1262
  17.8 2.1 fusion.1269
  19.9 2.1 fusion.1268
  22.0 2.1 fusion.1267
  24.1 2.1 fusion.1266
  26.2 1.3 slice.998
  27.5 1.9 fusion.1265
  29.4 2.1 fusion.1264
  31.5 0.7 copy.21
  32.2 0.1 reshape.233
  32.3 0.9 slice_bitcast_fusion.9
  33.1 24.4 %gather_fusion.2 = bf16[4096]{0:T(1024)(128)(2,1)S(1)} fusion(bf16[41]{0:T(256)(128)(2,1)S(1)} %get-tuple-element.7, s32[4096]{0:T(1024)S(1)} %broadcast_clamp_fusion), kind=kCustom, calls=%fused_computation.2 | custom fusion | bytes 32768 | tf_op jit(solution)/shard_map/gather | solution.py:47
  57.5 0.1 reshape.344
  57.6 24.4 %gather_fusion.1 = bf16[4096]{0:T(1024)(128)(2,1)S(1)} fusion(bf16[41]{0:T(256)(128)(2,1)S(1)} %get-tuple-element.8, s32[4096]{0:T(1024)S(1)} %broadcast_clamp_fusion), kind=kCustom, calls=%fused_computation.1 | custom fusion | bytes 32768 | tf_op jit(solution)/shard_map/gather | solution.py:47
  82.0 0.7 reshape.288
  82.7 24.4 %gather_fusion.3 = bf16[4096]{0:T(1024)(128)(2,1)S(1)} fusion(bf16[41]{0:T(256)(128)(2,1)S(1)} %get-tuple-element.10, s32[4096]{0:T(1024)S(1)} %broadcast_clamp_fusion), kind=kCustom, calls=%fused_computation.3 | custom fusion | bytes 32768 | tf_op jit(solution)/shard_map/gather | solution.py:47
  107.1 0.7 reshape.400
  107.8 24.4 %gather_fusion.4 = bf16[4096]{0:T(1024)(128)(2,1)S(1)} fusion(bf16[41]{0:T(256)(128)(2,1)S(1)} %get-tuple-element.9, s32[4096]{0:T(1024)S(1)} %broadcast_clamp_fusion), kind=kCustom, calls=%fused_computation.4 | custom fusion | bytes 32768 | tf_op jit(solution)/shard_map/gather | solution.py:47
  132.2 0.7 reshape.456
  132.9 24.6 %gather_fusion = bf16[4096]{0:T(1024)(128)(2,1)S(1)} fusion(bf16[41]{0:T(256)(128)(2,1)S(1)} %get-tuple-element.6, s32[4096]{0:T(1024)S(1)} %broadcast_clamp_fusion), kind=kCustom, calls=%fused_computation | custom fusion | bytes 32768 | tf_op jit(solution)/shard_map/gather | solution.py:47
  157.5 0.7 reshape.232
  158.2 0.1 broadcast_multiply_fusion
  158.3 0.1 multiply_add_fusion
  158.3 0.2 broadcast_add_fusion
  158.6 31.2 %convolution_multiply_fusion.2 = f32[64,2048]{1,0:T(8,128)} fusion(bf16[]{:T(256)} %bitcast.169, bf16[]{:T(256)} %bitcast.170, bf16[]{:T(256)} %bitcast.171, bf16[]{:T(256)} %bitcast.172, bf16[]{:T(256)} %bitcast.173, bf16[]{:T(256)} %bitcast.175, bf16[]{:T(256)} %bitcast.174, bf16[]{:T(256)} %bitcast.135, bf16[]{:T(256)} %bitcast.136, bf16[]{:T(256)} %bitcast.137, ...), kind=kOutput, calls=%fused_computation.519 | convolution fusion | flops 939810816 | bytes 1318994 | tf_op jit(solution)/shard_map/dot_general | solution.py:104
  189.8 31.2 %convolution_multiply_fusion.3 = f32[64,2048]{1,0:T(8,128)} fusion(bf16[]{:T(256)} %bitcast.125, bf16[]{:T(256)} %bitcast.126, bf16[]{:T(256)} %bitcast.127, bf16[]{:T(256)} %bitcast.128, bf16[]{:T(256)} %bitcast.129, bf16[]{:T(256)} %bitcast.131, bf16[]{:T(256)} %bitcast.130, bf16[]{:T(256)} %bitcast.91, bf16[]{:T(256)} %bitcast.92, bf16[]{:T(256)} %bitcast.93, ...), kind=kOutput, calls=%fused_computation.520 | convolution fusion | flops 939810816 | bytes 1318994 | tf_op jit(solution)/shard_map/dot_general | solution.py:104
  221.1 31.3 %convolution_multiply_fusion.1 = f32[64,2048]{1,0:T(8,128)} fusion(bf16[]{:T(256)} %bitcast.213, bf16[]{:T(256)} %bitcast.214, bf16[]{:T(256)} %bitcast.215, bf16[]{:T(256)} %bitcast.216, bf16[]{:T(256)} %bitcast.217, bf16[]{:T(256)} %bitcast.219, bf16[]{:T(256)} %bitcast.218, bf16[]{:T(256)} %bitcast.179, bf16[]{:T(256)} %bitcast.180, bf16[]{:T(256)} %bitcast.181, ...), kind=kOutput, calls=%fused_computation.518 | convolution fusion | flops 939810816 | bytes 1318994 | tf_op jit(solution)/shard_map/dot_general | solution.py:104
  252.4 31.1 %convolution_multiply_fusion = f32[64,2048]{1,0:T(8,128)} fusion(bf16[]{:T(256)} %bitcast.257, bf16[]{:T(256)} %bitcast.258, bf16[]{:T(256)} %bitcast.259, bf16[]{:T(256)} %bitcast.260, bf16[]{:T(256)} %bitcast.261, bf16[]{:T(256)} %bitcast.263, bf16[]{:T(256)} %bitcast.262, bf16[]{:T(256)} %bitcast.223, bf16[]{:T(256)} %bitcast.224, bf16[]{:T(256)} %bitcast.225, ...), kind=kOutput, calls=%fused_computation.517 | convolution fusion | flops 939810816 | bytes 1318994 | tf_op jit(solution)/shard_map/dot_general | solution.py:104
  283.5 0.0 copy-start.9
  283.5 31.7 %fusion.589 = bf16[64,2048]{1,0:T(8,128)(2,1)S(1)} fusion(f32[64,2048]{1,0:T(8,128)} %convolution_multiply_fusion, f32[64,2048]{1,0:T(8,128)} %convolution_multiply_fusion.1, f32[64,2048]{1,0:T(8,128)} %convolution_multiply_fusion.2, f32[64,2048]{1,0:T(8,128)} %convolution_multiply_fusion.3, bf16[]{:T(256)} %bitcast.80, bf16[]{:T(256)} %bitcast.81, ...), kind=kOutput, calls=%fused_computation.526 | convolution fusion | flops 940466176 | bytes 3154002 | tf_op jit(solution)/shard_map/dot_general | solution.py:104
  315.3 0.0 copy-start.10
  315.3 120.3 %fusion.598 = bf16[8,8,16,128]{3,1,2,0:T(8,128)(2,1)S(1)} fusion(bf16[64,2048]{1,0:T(8,128)(2,1)S(1)} %fusion.589, f32[2048]{0:T(1024)S(1)} %bitcast.2416, s32[2048]{0:T(1024)S(1)} %bitcast.2417, f32[64]{0:T(128)S(1)} %bitcast.2418, s32[64]{0:T(128)S(1)} %bitcast.2419), kind=kOutput, calls=%fused_computation.573 | convolution fusion | flops 616886272 | bytes 541184 | tf_op jit(solution)/shard_map/dot_general | solution.py:110
  436.3 1.4 scatter_fusion
  437.7 8.1 fusion.761
  445.8 0.0 all-reduce.4.cloned.1.call-update
  445.9 0.1 reshape.229
  446.0 0.5 copy-done.12
  446.5 0.6 dynamic-slice
  447.1 125.9 %all-reduce.1 = f32[32,16]{1,0:T(8,128)S(1)} all-reduce(f32[32,16]{1,0:T(8,128)S(1)} %reshape.229), channel_id=3, replica_groups=mesh['visit'=32,'sky'=8] {'visit'}, use_global_device_ids=true, to_apply=%region_3.4.clone | all-reduce | flops 512 | bytes 4096
  573.0 0.7 fusion.811
  573.6 200.1 %all-reduce.4.cloned.1.call-done = f32[32,16,64,128]{3,1,0,2:T(8,128)} async-done(((f32[32,16,64,128]{3,1,0,2:T(8,128)}), f32[32,16,64,128]{3,1,0,2:T(8,128)}) %all-reduce.4.cloned.1.call-update) | async-done | bytes 16777232
  773.7 1.8 fusion.760
  775.5 0.2 copy.20
  775.7 0.0 copy-start.1
  775.7 0.1 fusion.1258
  775.8 1.5 collective-permute-start
  777.3 1.3 collective-permute-start.1
  778.6 0.7 fusion.1270
  779.3 2.6 collective-permute-done.1
  781.9 0.3 concatenate.52
  782.3 5.1 collective-permute-start.2
  787.4 1.9 collective-permute-start.3
  789.4 0.7 fusion.1272
  790.0 0.6 multiply_reduce_fusion
  790.7 0.7 fusion.1271
  791.4 3.2 collective-permute-done.3
  794.5 29.5 %fusion.604 = f32[64,2088]{1,0:T(8,128)S(1)} fusion(f32[64,2088]{1,0:T(8,128)S(1)} %concatenate.52, f32[20,2088]{1,0:T(8,128)S(1)} %collective-permute-done.3, f32[20,2088]{1,0:T(8,128)S(1)} %collective-permute-done.2, f32[]{:T(128)} %bitcast.312, f32[]{:T(128)} %bitcast.311, f32[]{:T(128)} %bitcast.310, f32[]{:T(128)} %bitcast.309, f32[]{:T(128)} %bitcast.308, ...), kind=kLoop, calls=%fused_computation.577 | loop fusion | flops 16169472 | bytes 1403300 | tf_op jit(solution)/shard_map/add | solution.py:61
  824.0 32.5 %fusion.720 = f32[64,2048]{1,0:T(8,128)} fusion(f32[64,2088]{1,0:T(8,128)S(1)} %fusion.604, f32[]{:T(128)} %multiply_reduce_fusion, f32[]{:T(128)} %bitcast.312, f32[]{:T(128)} %bitcast.311, f32[]{:T(128)} %bitcast.310, f32[]{:T(128)} %bitcast.309, f32[]{:T(128)} %bitcast.308, f32[]{:T(128)} %bitcast.307, f32[]{:T(128)} %bitcast.306, f32[]{:T(128)} %bitcast.305, ...), kind=kLoop, calls=%fused_computation.697 | loop fusion | flops 10747904 | bytes 22020264 | tf_op jit(solution)/shard_map/div | solution.py:149
  (35 shorter events, 0.2 us)
Async XLA Ops:
  7.2 151.4 %copy-start = (bf16[1,64,2048]{2,1,0:T(8,128)(2,1)S(1)}, bf16[1,64,2048]{2,1,0:T(8,128)(2,1)}, u32[]{:S(2)}) copy-start(bf16[1,64,2048]{2,1,0:T(8,128)(2,1)} %param.11) | copy-start | bytes 786436
  7.2 766.5 %all-reduce.4.cloned.1.call-start = ((), (), s32[]{:S(2)}) async-start(), calls=%async_computation | async-start | bytes 33554432
  158.6 31.2 %copy-start.5 = (bf16[64,64]{1,0:T(8,128)(2,1)S(1)}, bf16[64,64]{1,0:T(8,128)(2,1)}, u32[]{:S(2)}) copy-start(bf16[64,64]{1,0:T(8,128)(2,1)} %reshape.288) | copy-start | bytes 24580
  189.8 31.2 %copy-start.4 = (bf16[64,64]{1,0:T(8,128)(2,1)S(1)}, bf16[64,64]{1,0:T(8,128)(2,1)}, u32[]{:S(2)}) copy-start(bf16[64,64]{1,0:T(8,128)(2,1)} %reshape.400) | copy-start | bytes 24580
  221.1 31.3 %copy-start.3 = (bf16[64,64]{1,0:T(8,128)(2,1)S(1)}, bf16[64,64]{1,0:T(8,128)(2,1)}, u32[]{:S(2)}) copy-start(bf16[64,64]{1,0:T(8,128)(2,1)} %reshape.456) | copy-start | bytes 24580
  252.4 31.1 %copy-start.2 = (bf16[64,64]{1,0:T(8,128)(2,1)S(1)}, bf16[64,64]{1,0:T(8,128)(2,1)}, u32[]{:S(2)}) copy-start(bf16[64,64]{1,0:T(8,128)(2,1)} %reshape.232) | copy-start | bytes 24580
  283.5 31.7 %copy-start.6 = (f32[1,2048]{1,0:T(1,128)S(1)}, f32[1,2048]{1,0:T(1,128)}, u32[]{:S(2)}) copy-start(f32[1,2048]{1,0:T(1,128)} %param.16) | copy-start | bytes 24580
  283.5 31.7 %copy-start.7 = (s32[1,2048]{1,0:T(1,128)S(1)}, s32[1,2048]{1,0:T(1,128)}, u32[]{:S(2)}) copy-start(s32[1,2048]{1,0:T(1,128)} %param.15) | copy-start | bytes 24580
  283.5 31.8 %copy-start.8 = (f32[1,64]{1,0:T(1,128)S(1)}, f32[1,64]{1,0:T(1,128)}, u32[]{:S(2)}) copy-start(f32[1,64]{1,0:T(1,128)} %param.18) | copy-start | bytes 772
  283.5 31.8 %copy-start.9 = (s32[1,64]{1,0:T(1,128)S(1)}, s32[1,64]{1,0:T(1,128)}, u32[]{:S(2)}) copy-start(s32[1,64]{1,0:T(1,128)} %param.17) | copy-start | bytes 772
  315.3 121.0 %copy-start.10 = (s32[1,16]{1,0:T(1,128)S(1)}, s32[1,16]{1,0:T(1,128)}, u32[]{:S(2)}) copy-start(s32[1,16]{1,0:T(1,128)} %param.21) | copy-start | bytes 196
  315.3 121.0 %copy-start.11 = (s32[1,16,1]{1,2,0:T(1,128)S(1)}, s32[1,16,1]{1,2,0:T(1,128)}, u32[]{:S(2)}) copy-start(s32[1,16,1]{1,2,0:T(1,128)} %param.20) | copy-start | bytes 196
  445.8 0.7 copy-start.12
  775.7 80.8 %copy-start.1 = (f32[8,8,16,128]{3,1,2,0:T(8,128)}, f32[8,8,16,128]{3,1,2,0:T(8,128)S(1)}, u32[]{:S(2)}) copy-start(f32[8,8,16,128]{3,1,2,0:T(8,128)S(1)} %copy.20) | copy-start | bytes 1572868
  775.8 3.5 collective-permute-start
  777.3 4.7 collective-permute-start.1
  782.3 9.1 %collective-permute-start.2 = (f32[20,2088]{1,0:T(8,128)S(1)}, f32[20,2088]{1,0:T(8,128)S(1)}, u32[]{:S(2)}, u32[]{:S(2)}) collective-permute-start(f32[20,2088]{1,0:T(8,128)S(1)} %get-tuple-element.2), channel_id=1, source_target_pairs={{0,1},{1,2},{2,3},{3,4},{4,5},{5,6},{6,7},{8,9},{9,10},{10,11},{11... | collective-permute-start | bytes 501128 | tf_op jit(solution)/shard_map/ppermute | solution.py:17
  787.4 7.1 collective-permute-start.3
Sparse Core Ops, SparseCore 0:
  446.0 327.6 all-reduce.3
where the time goes:
time: 871 us; the launch traced here: 864 us
  matrix products  285 us (33%)
  waiting for transfers between devices  206 us (24%)
  local copies, waits for them, and re-layouts  156 us (18%)
  blocking collectives  126 us (14%)
  other arithmetic  65.5 us (8%)
  between operations  15.3 us (2%)
  starting transfers between devices  9.85 us (1%)
    unnamed x2, waiting for transfers between devices  200 us
    dot_general x5, matrix products, local(): jnp.dot(col_bands[basis_idx], across, preferred_element_type=jnp.float32)  157 us
    gather x22, local copies, waits for them, and re-layouts, band_matrix(): tap_values[jnp.clip(offset, 0, KW - 1)]  149 us
    unnamed x1, blocking collectives  126 us
    dot_general x1, matrix products, local(): jnp.dot(warp_rows, col_warped, preferred_element_type=jnp.float32)  120 us
    div x1, other arithmetic, local(): return (coadded, smoothed / noise_norm)  32.5 us
    add x1, other arithmetic, filter_rows(): result = result + smooth_taps[offset] * padded[offset:offset + out_rows, :]  29.5 us
  transfers between devices with their start and end apart: 5, of which 3 were waited for; matrix products, arithmetic and copies ran while one was open for 0% of the time, Pallas kernels for 0%

commit v1 on v0

v1 whole, which is shorter than its diff:
```python
import jax
import jax.numpy as jnp
from jax import lax
from jax.experimental import pallas as pl
from jax.experimental.pallas import tpu as pltpu
from jax.sharding import PartitionSpec as P

R = 64
W = 2048
NB = 5
KW = 41
HALO = 20
SPT = 16
SLOTS = 2
LANES = 128
META = 16
MSG = SLOTS * R + META
NT = (((1,), (1,)), ((), ()))
TN = (((0,), (0,)), ((), ()))
BF = jnp.bfloat16
F32 = jnp.float32


def dot(left, right, dims=(((1,), (0,)), ((), ())), precision=None):
    return lax.dot_general(left, right, dims, preferred_element_type=F32, precision=precision)


def toeplitz(row, rows, shift=LANES - HALO):
    row = pltpu.roll(row, shift % 8, 1) if shift % 8 else row
    return pltpu.roll(jnp.broadcast_to(row, (rows, row.shape[1])), shift // 8 * 8, 1, stride=1, stride_axis=0)


def lanczos(offset):
    return (
        3.0
        * jnp.sin(jnp.pi * offset)
        * jnp.sin(jnp.pi * offset / 3.0)
        / (jnp.pi * jnp.pi * offset * offset)
    )


def lanczos_weights(frac):
    shape = (8, frac.shape[1])
    shift = lax.broadcasted_iota(jnp.int32, shape, 0) - 2
    return lanczos(jnp.broadcast_to(frac, shape) - shift.astype(F32)).astype(BF).astype(F32)


def tile_kernel(
    coeff_ref, weight_ref, owner_ref, block_ref,
    tile_ref, row_taps_ref, col_taps_ref, start_x_ref, frac_x_ref, start_y_ref, frac_y_ref,
    out_ref,
    taps_ref, stack_ref, matched_ref, shifted_ref, col_ref, count_ref,
):
    taps_ref[...] = jnp.zeros_like(taps_ref)
    taps_ref[0:NB, 0:KW] = row_taps_ref[...].astype(F32)
    taps_ref[8:8 + NB, 0:KW] = col_taps_ref[...].astype(F32)
    row_band = jnp.concatenate([toeplitz(taps_ref[k:k + 1, :], LANES) for k in range(NB)], axis=0).astype(BF)
    col_bands = [toeplitz(taps_ref[8 + k:9 + k, 0:LANES], R)[:, 0:R].astype(BF) for k in range(NB)]
    stack_ref[0:R, :] = jnp.zeros((R, LANES), BF)
    stack_ref[(SPT + 1) * R:(SPT + 2) * R, :] = jnp.zeros((R, LANES), BF)
    for s in range(SPT):
        stack_ref[(s + 1) * R:(s + 2) * R, :] = tile_ref[0, :, s * LANES:(s + 1) * LANES]
    group = 4
    width = group * LANES
    for g in range(SPT // group):
        first = g * group * R
        rows = group * R
        window = jnp.concatenate(
            [stack_ref[first + j * R:first + j * R + rows, :] for j in range(3)], axis=1
        )
        across = dot(window, row_band, NT).astype(BF)
        column = lax.broadcasted_iota(jnp.int32, (1, width), 1) + g * width
        x_coord = (2 * column - (W - 1)).astype(F32) / (W - 1)
        row = lax.broadcasted_iota(jnp.int32, (R, 1), 0)
        y_coord = (2 * row - (R - 1)).astype(F32) / (R - 1)
        matched = jnp.zeros((R, width), F32)
        for k in range(NB):
            term = jnp.concatenate(
                [across[j * R:(j + 1) * R, k * LANES:(k + 1) * LANES] for j in range(group)], axis=1
            )
            basis_term = dot(col_bands[k], term)
            coeff_map = coeff_ref[0, k, 0] + coeff_ref[0, k, 1] * x_coord + coeff_ref[0, k, 2] * y_coord
            matched = matched + coeff_map * basis_term
        matched_ref[:, g * width:(g + 1) * width] = matched.astype(BF).astype(F32)
    for s in range(6):
        shift = (2 - s) % W
        value = matched_ref[...]
        shifted_ref[s * R:(s + 1) * R, :] = (value if shift == 0 else pltpu.roll(value, shift, 1)).astype(BF)
    weights_x = lanczos_weights(frac_x_ref[...])
    chunk = 256
    for c in range(W // chunk):
        cols = slice(c * chunk, (c + 1) * chunk)
        source = lax.broadcasted_iota(jnp.int32, (W, chunk), 0)
        chosen = (source == start_x_ref[:, cols]).astype(F32).astype(BF)
        taken = dot(shifted_ref[...], chosen)
        total = weights_x[0:1, cols] * taken[0:R]
        for s in range(1, 6):
            total = total + weights_x[s:s + 1, cols] * taken[s * R:(s + 1) * R]
        col_ref[:, cols] = total.astype(BF)
    weights_y = lanczos_weights(frac_y_ref[...])
    step = lax.broadcasted_iota(jnp.int32, (R, R), 0) - start_y_ref[...]
    warp_y = jnp.zeros((R, R), F32)
    for s in range(6):
        warp_y = jnp.where(step == s - 2, weights_y[s:s + 1, :], warp_y)
    warped = dot(warp_y.T.astype(BF), col_ref[...]).astype(BF)
    out_ref[...] = jnp.zeros_like(out_ref)
    for o in range(out_ref.shape[0]):
        count_ref[o] = 0
    weight = weight_ref[...].astype(F32)
    row = lax.broadcasted_iota(jnp.int32, (META, LANES), 0)
    slot_of = lax.broadcasted_iota(jnp.int32, (META, LANES), 1) // META
    for s in range(SPT):
        owner = owner_ref[0, s, 0]
        slot = count_ref[owner]
        count_ref[owner] = slot + 1
        out_ref[owner, pl.ds(pl.multiple_of(slot * R, R), R), :] = warped[:, s * LANES:(s + 1) * LANES]
        note = jnp.where(row == 0, weight, jnp.where(row == 1, block_ref[0, s].astype(F32), 0.0))
        note = jnp.where(slot_of == slot, note, 0.0)
        held = out_ref[owner, SLOTS * R:MSG, :].astype(F32)
        out_ref[owner, SLOTS * R:MSG, :] = (held + note).astype(BF)


def sum_kernel(in_ref, coadd_ref):
    peers = in_ref.shape[0]
    depth = peers * SLOTS * META
    notes = []
    per_row = LANES // (SLOTS * META)
    for q in range(peers // per_row):
        total = None
        for j in range(per_row):
            note = in_ref[q * per_row + j, SLOTS * R:MSG, :].astype(F32)
            note = pltpu.roll(note, j * SLOTS * META, 1) if j else note
            total = note if total is None else total + note
        notes.append(total)
    notes = jnp.concatenate(notes, axis=1)
    weight, block = notes[0:1], notes[1:2]
    same = (
        lax.broadcasted_iota(jnp.int32, (META, depth), 0)
        == lax.broadcasted_iota(jnp.int32, (META, depth), 1) % META
    )
    spread = jnp.concatenate(
        [jnp.where(same, jnp.where(block == b, weight, 0.0), 0.0) for b in range(SPT)], axis=0
    ).astype(BF)
    parts = []
    for g in range(R // META):
        pieces = [
            in_ref[v, slot * R + g * META:slot * R + (g + 1) * META, :]
            for v in range(peers) for slot in range(SLOTS)
        ]
        parts.append(jnp.concatenate(pieces, axis=0))
    parts.append(jnp.ones((depth, LANES), BF))
    total = dot(spread, jnp.concatenate(parts, axis=1))
    scale = 1.0 / (total[:, R // META * LANES:] + 1.0)
    for b in range(SPT):
        for g in range(R // META):
            rows = slice(b * META, (b + 1) * META)
            coadd_ref[g * META:(g + 1) * META, b * LANES:(b + 1) * LANES] = (
                total[rows, g * LANES:(g + 1) * LANES] * scale[rows]
            )


def taper_row(width, scale=1.0):
    lane = lax.broadcasted_iota(jnp.int32, (1, width), 1)
    at = (lane - HALO).astype(F32) / 21.0
    return jnp.where(lane < KW, (1.0 - at * at) * scale, 0.0)


def across_kernel(coadd_ref, left_ref, right_ref, out_ref, stack_ref):
    band = toeplitz(taper_row(3 * LANES), LANES)
    stack_ref[0:R, :] = left_ref[...]
    stack_ref[(SPT + 1) * R:(SPT + 2) * R, :] = right_ref[...]
    for s in range(SPT):
        stack_ref[(s + 1) * R:(s + 2) * R, :] = coadd_ref[:, s * LANES:(s + 1) * LANES]
    window = jnp.concatenate([stack_ref[j * R:(j + SPT) * R, :] for j in range(3)], axis=1)
    total = dot(window, band, NT, lax.Precision.HIGHEST)
    for s in range(SPT):
        out_ref[:, s * LANES:(s + 1) * LANES] = total[s * R:(s + 1) * R, :]


EDGE = 24


def down_kernel(mid_ref, above_ref, below_ref, out_ref):
    norm = sum((1.0 - (a / 21.0) ** 2) ** 2 for a in range(-HALO, HALO + 1))
    band = toeplitz(taper_row(LANES, 1.0 / norm), R, EDGE - HALO)
    rows = jnp.concatenate([above_ref[...], mid_ref[...], below_ref[...]], axis=0)
    out_ref[...] = dot(band[:, 0:R + 2 * EDGE], rows, precision=lax.Precision.HIGHEST)


def vmem(n):
    return [pl.BlockSpec(memory_space=pltpu.VMEM)] * n


def smem(n):
    return [pl.BlockSpec(memory_space=pltpu.SMEM)] * n


PARAMS = pltpu.CompilerParams(vmem_limit_bytes=40 * 1024 * 1024)


def neighbours(axis):
    size = lax.axis_size(axis)
    up = [(i, i + 1) for i in range(size - 1)]
    return up, [(j, i) for i, j in up]


def local(
    ccd_tiles, row_taps, col_taps, psf_coeffs, warp_start_x, warp_frac_x, warp_start_y, warp_frac_y,
    tile_weight, strip_owner, strip_block,
):
    peers = lax.axis_size("visit")
    messages = pl.pallas_call(
        tile_kernel,
        out_shape=jax.ShapeDtypeStruct((peers, MSG, LANES), BF),
        in_specs=smem(1) + vmem(1) + smem(2) + vmem(7),
        out_specs=pl.BlockSpec(memory_space=pltpu.VMEM),
        scratch_shapes=[
            pltpu.VMEM((16, 3 * LANES), F32),
            pltpu.VMEM(((SPT + 2) * R, LANES), BF),
            pltpu.VMEM((R, W), F32),
            pltpu.VMEM((6 * R, W), BF),
            pltpu.VMEM((R, W), BF),
            pltpu.SMEM((peers,), jnp.int32),
        ],
        compiler_params=PARAMS,
    )(
        psf_coeffs, tile_weight.reshape(1, 1), strip_owner, strip_block,
        ccd_tiles, row_taps, col_taps, warp_start_x, warp_frac_x, warp_start_y, warp_frac_y,
    )
    received = lax.all_to_all(messages, "visit", 0, 0, tiled=True)
    coadd = pl.pallas_call(
        sum_kernel,
        out_shape=jax.ShapeDtypeStruct((R, W), F32),
        in_specs=vmem(1),
        out_specs=pl.BlockSpec(memory_space=pltpu.VMEM),
        compiler_params=PARAMS,
    )(received)
    up, down = neighbours("visit")
    left = lax.ppermute(coadd[:, W - LANES:], "visit", up)
    right = lax.ppermute(coadd[:, :LANES], "visit", down)
    mid = pl.pallas_call(
        across_kernel,
        out_shape=jax.ShapeDtypeStruct((R, W), F32),
        in_specs=vmem(3),
        out_specs=pl.BlockSpec(memory_space=pltpu.VMEM),
        scratch_shapes=[pltpu.VMEM(((SPT + 2) * R, LANES), F32)],
        compiler_params=PARAMS,
    )(coadd, left, right)
    up, down = neighbours("sky")
    above = lax.ppermute(mid[R - EDGE:], "sky", up)
    below = lax.ppermute(mid[:EDGE], "sky", down)
    detection = pl.pallas_call(
        down_kernel,
        out_shape=jax.ShapeDtypeStruct((R, W), F32),
        in_specs=vmem(3),
        out_specs=pl.BlockSpec(memory_space=pltpu.VMEM),
        compiler_params=PARAMS,
    )(mid, above, below)
    return coadd, detection


def solution(mesh):
    tiles = ("visit", "sky")
    in_specs = (
        P(tiles, None, None),
        P(),
        P(),
        P(tiles, None, None),
        P(tiles, None),
        P(tiles, None),
        P(tiles, None),
        P(tiles, None),
        P(tiles),
        P(tiles, None, None),
        P(tiles, None),
    )
    out_specs = (P("sky", "visit"), P("sky", "visit"))
    return jax.shard_map(local, mesh=mesh, in_specs=in_specs, out_specs=out_specs, check_vma=False)
```

time: 871 us -> 84.9 us (0.10)
  the two profiles are of different devices: /device:TPU:1 before, /device:TPU:10 now
where the time goes in v1:
time: 84.9 us; the launch traced here: 84.3 us
  blocking collectives  43.2 us (51%)
  Pallas kernels  11.2 us (13%)
  starting transfers between devices  10.2 us (12%)
  waiting for transfers between devices  9.39 us (11%)
  local copies, waits for them, and re-layouts  9.02 us (11%)
  between operations  1.35 us (2%)
    all_to_all x1, blocking collectives, local(): received = lax.all_to_all(messages, 'visit', 0, 0, tiled=True)  43.2 us
    unnamed x20, local copies, waits for them, and re-layouts  8.21 us
    pallas_call x1, Pallas kernels, local(): pl.pallas_call(tile_kernel, out_shape=jax.ShapeDtypeStruct((peers, MSG, L...  6.72 us
    ppermute x1, waiting for transfers between devices, local(): left = lax.ppermute(coadd[:, W - LANES:], 'visit', up)  4.82 us
    ppermute x1, waiting for transfers between devices, local(): above = lax.ppermute(mid[R - EDGE:], 'sky', up)  3.82 us
    ppermute x1, starting transfers between devices, local(): left = lax.ppermute(coadd[:, W - LANES:], 'visit', up)  3.08 us
    ppermute x1, starting transfers between devices, local(): right = lax.ppermute(coadd[:, :LANES], 'visit', down)  2.75 us
    ppermute x1, starting transfers between devices, local(): above = lax.ppermute(mid[R - EDGE:], 'sky', up)  2.41 us
  transfers between devices with their start and end apart: 4, of which 3 were waited for; matrix products, arithmetic and copies ran while one was open for 0% of the time, Pallas kernels for 0%

profile of v1, /device:TPU:10, one launch (start us, length us, event | category | flops | bytes accessed | tf_op | source)
XLA Modules:
  0.0 84.3 jit_solution(4980442206555113222)
XLA Ops:
  1.3 0.8 copy.13.coeff_ref
  2.1 0.7 copy.14.owner_ref
  2.8 0.0 copy-start.1
  2.8 0.9 %copy-done.1 = bf16[1,64,2048]{2,1,0:T(8,128)(2,1)S(1)} copy-done((bf16[1,64,2048]{2,1,0:T(8,128)(2,1)S(1)}, bf16[1,64,2048]{2,1,0:T(8,128)(2,1)}, u32[]{:S(2)}) %copy-start.1) | copy-done | bytes 262168
  3.7 0.0 copy-start.2
  3.7 0.7 copy-done.2
  4.4 0.0 copy-start.3
  4.4 0.7 copy-done.3
  5.1 0.0 copy-start.4
  5.1 0.7 copy-done.4
  5.8 0.0 copy-start.5
  5.8 0.7 copy-done.5
  6.5 0.0 copy-start.6
  6.5 0.7 copy-done.6
  7.1 0.0 copy-start.7
  7.2 0.7 copy-done.7
  7.8 0.0 copy-start.8
  7.8 0.7 copy-done.8
  8.5 6.7 %shard_map.122 = bf16[32,144,128]{2,1,0:T(8,128)(2,1)S(1)} custom-call(f32[1,5,3]{2,1,0:T(8,128)S(1)} %copy.13.coeff_ref, bf16[1,1]{1,0:T(2,128)(2,1)} %bitcast.1.weight_ref, s32[1,16,1]{2,1,0:T(8,128)S(1)} %copy.14.owner_ref, s32[1,16]{1,0:T(1,128)S(1)} %copy-done.6, bf16[1,64,2048]{2,1,0:T(8,128)(2,1)S(1)} %copy-done.1, bf16[5,41]{1,0:T(8,128)(2,1)S(1)} %copy-done.4, ...), custom_call_target="tpu_custom_call" | custom-call | tf_op jit(solution)/shard_map/pallas_call | solution.py:212
  15.2 43.2 %all_to_all.5.in_ref = bf16[32,144,128]{2,1,0:T(8,128)(2,1)S(1)} all-to-all(bf16[32,144,128]{2,1,0:T(8,128)(2,1)S(1)} %shard_map.122), channel_id=1, replica_groups=mesh['visit'=32,'sky'=8] {'visit'}, dimensions={0} | all-to-all | bytes 2359296 | tf_op jit(solution)/shard_map/all_to_all | solution.py:230
  58.4 1.4 %shard_map.123.coadd_ref = f32[64,2048]{1,0:T(8,128)} custom-call(bf16[32,144,128]{2,1,0:T(8,128)(2,1)S(1)} %all_to_all.5.in_ref), custom_call_target="tpu_custom_call" | custom-call | tf_op jit(solution)/shard_map/pallas_call | solution.py:231
  59.8 0.8 fusion.1
  60.6 2.7 %collective-permute-start.1 = (f32[64,128]{1,0:T(8,128)S(1)}, f32[64,128]{1,0:T(8,128)S(1)}, u32[]{:S(2)}, u32[]{:S(2)}) collective-permute-start(f32[64,128]{1,0:T(8,128)S(1)} %get-tuple-element.4), channel_id=1, source_target_pairs={{8,0},{16,8},{24,16},{32,24},{40,32},{48,40},{56,48},{64,56},{72,6... | collective-permute-start | bytes 98312 | tf_op jit(solution)/shard_map/ppermute | solution.py:240
  63.3 3.1 %collective-permute-start = (f32[64,128]{1,0:T(8,128)S(1)}, f32[64,128]{1,0:T(8,128)S(1)}, u32[]{:S(2)}, u32[]{:S(2)}) collective-permute-start(f32[64,128]{1,0:T(8,128)S(1)} %get-tuple-element.5), channel_id=1, source_target_pairs={{0,8},{8,16},{16,24},{24,32},{32,40},{40,48},{48,56},{56,64},{64,7... | collective-permute-start | bytes 98312 | tf_op jit(solution)/shard_map/ppermute | solution.py:239
  66.4 0.0 collective-permute-done.1.right_ref
  66.5 4.8 %collective-permute-done.left_ref = f32[64,128]{1,0:T(8,128)S(1)} collective-permute-done((f32[64,128]{1,0:T(8,128)S(1)}, f32[64,128]{1,0:T(8,128)S(1)}, u32[]{:S(2)}, u32[]{:S(2)}) %collective-permute-start) | collective-permute-done | bytes 32800 | tf_op jit(solution)/shard_map/ppermute | solution.py:239
  71.3 0.0 copy-start
  71.3 1.0 %copy-done = f32[64,2048]{1,0:T(8,128)S(1)} copy-done((f32[64,2048]{1,0:T(8,128)S(1)}, f32[64,2048]{1,0:T(8,128)}, u32[]{:S(2)}) %copy-start) | copy-done | bytes 524312
  72.3 1.6 %shard_map.124.mid_ref = f32[64,2048]{1,0:T(8,128)S(1)} custom-call(f32[64,2048]{1,0:T(8,128)S(1)} %copy-done, f32[64,128]{1,0:T(8,128)S(1)} %collective-permute-done.left_ref, f32[64,128]{1,0:T(8,128)S(1)} %collective-permute-done.1.right_ref), custom_call_target="tpu_custom_call" | custom-call | tf_op jit(solution)/shard_map/pallas_call | solution.py:241
  73.9 1.9 %collective-permute-start.3 = (f32[24,2048]{1,0:T(8,128)S(1)}, f32[24,2048]{1,0:T(8,128)S(1)}, u32[]{:S(2)}, u32[]{:S(2)}) collective-permute-start(f32[24,2048]{1,0:T(8,128)S(1)} %get-tuple-element.2), channel_id=1, source_target_pairs={{1,0},{2,1},{3,2},{4,3},{5,4},{6,5},{7,6},{9,8},{10,9},{11,10},{12... | collective-permute-start | bytes 589832 | tf_op jit(solution)/shard_map/ppermute | solution.py:251
  75.9 2.4 %collective-permute-start.2 = (f32[24,2048]{1,0:T(8,128)S(1)}, f32[24,2048]{1,0:T(8,128)S(1)}, u32[]{:S(2)}, u32[]{:S(2)}) collective-permute-start(f32[24,2048]{1,0:T(8,128)S(1)} %get-tuple-element.3), channel_id=1, source_target_pairs={{0,1},{1,2},{2,3},{3,4},{4,5},{5,6},{6,7},{8,9},{9,10},{10,11},{11... | collective-permute-start | bytes 589832 | tf_op jit(solution)/shard_map/ppermute | solution.py:250
  78.3 0.8 collective-permute-done.3.below_ref
  79.0 3.8 %collective-permute-done.2.above_ref = f32[24,2048]{1,0:T(8,128)S(1)} collective-permute-done((f32[24,2048]{1,0:T(8,128)S(1)}, f32[24,2048]{1,0:T(8,128)S(1)}, u32[]{:S(2)}, u32[]{:S(2)}) %collective-permute-start.2) | collective-permute-done | bytes 196640 | tf_op jit(solution)/shard_map/ppermute | solution.py:250
  82.8 1.5 %shard_map.125 = f32[64,2048]{1,0:T(8,128)} custom-call(f32[64,2048]{1,0:T(8,128)S(1)} %shard_map.124.mid_ref, f32[24,2048]{1,0:T(8,128)S(1)} %collective-permute-done.2.above_ref, f32[24,2048]{1,0:T(8,128)S(1)} %collective-permute-done.3.below_ref), custom_call_target="tpu_custom_call" | custom-call | tf_op jit(solution)/shard_map/pallas_call | solution.py:252
  (1 shorter events, 0.0 us)
Async XLA Ops:
  2.8 0.9 %copy-start.1 = (bf16[1,64,2048]{2,1,0:T(8,128)(2,1)S(1)}, bf16[1,64,2048]{2,1,0:T(8,128)(2,1)}, u32[]{:S(2)}) copy-start(bf16[1,64,2048]{2,1,0:T(8,128)(2,1)} %tile_ref.1) | copy-start | bytes 786436
  3.7 0.7 copy-start.2
  4.4 0.7 copy-start.3
  5.1 0.7 copy-start.4
  5.8 0.7 copy-start.5
  6.5 0.7 copy-start.6
  7.1 0.7 copy-start.7
  7.8 0.7 copy-start.8
  60.6 5.8 %collective-permute-start.1 = (f32[64,128]{1,0:T(8,128)S(1)}, f32[64,128]{1,0:T(8,128)S(1)}, u32[]{:S(2)}, u32[]{:S(2)}) collective-permute-start(f32[64,128]{1,0:T(8,128)S(1)} %get-tuple-element.4), channel_id=1, source_target_pairs={{8,0},{16,8},{24,16},{32,24},{40,32},{48,40},{56,48},{64,56},{72,6... | collective-permute-start | bytes 98312 | tf_op jit(solution)/shard_map/ppermute | solution.py:240
  63.3 7.9 %collective-permute-start = (f32[64,128]{1,0:T(8,128)S(1)}, f32[64,128]{1,0:T(8,128)S(1)}, u32[]{:S(2)}, u32[]{:S(2)}) collective-permute-start(f32[64,128]{1,0:T(8,128)S(1)} %get-tuple-element.5), channel_id=1, source_target_pairs={{0,8},{8,16},{16,24},{24,32},{32,40},{40,48},{48,56},{56,64},{64,7... | collective-permute-start | bytes 98312 | tf_op jit(solution)/shard_map/ppermute | solution.py:239
  71.3 1.0 %copy-start = (f32[64,2048]{1,0:T(8,128)S(1)}, f32[64,2048]{1,0:T(8,128)}, u32[]{:S(2)}) copy-start(f32[64,2048]{1,0:T(8,128)} %shard_map.123.coadd_ref) | copy-start | bytes 1572868
  73.9 5.1 %collective-permute-start.3 = (f32[24,2048]{1,0:T(8,128)S(1)}, f32[24,2048]{1,0:T(8,128)S(1)}, u32[]{:S(2)}, u32[]{:S(2)}) collective-permute-start(f32[24,2048]{1,0:T(8,128)S(1)} %get-tuple-element.2), channel_id=1, source_target_pairs={{1,0},{2,1},{3,2},{4,3},{5,4},{6,5},{7,6},{9,8},{10,9},{11,10},{12... | collective-permute-start | bytes 589832 | tf_op jit(solution)/shard_map/ppermute | solution.py:251
  75.9 7.0 %collective-permute-start.2 = (f32[24,2048]{1,0:T(8,128)S(1)}, f32[24,2048]{1,0:T(8,128)S(1)}, u32[]{:S(2)}, u32[]{:S(2)}) collective-permute-start(f32[24,2048]{1,0:T(8,128)S(1)} %get-tuple-element.3), channel_id=1, source_target_pairs={{0,1},{1,2},{2,3},{3,4},{4,5},{5,6},{6,7},{8,9},{9,10},{10,11},{11... | collective-permute-start | bytes 589832 | tf_op jit(solution)/shard_map/ppermute | solution.py:250

commit v2 on v1

v2 whole, which is shorter than its diff:
```python
import jax
import jax.numpy as jnp
from jax import lax
from jax.experimental import pallas as pl
from jax.experimental.pallas import tpu as pltpu
from jax.sharding import PartitionSpec as P

R = 64
W = 2048
NB = 5
KW = 41
HALO = 20
SPT = 16
SLOTS = 2
LANES = 128
UNIT = 16
NOTE = SLOTS * R
MSG = NOTE + 2 * UNIT
NOTE_LANES = 2 * UNIT
LEFT_AT = (32, 80)
RIGHT_AT = (52, 100)
EDGE = 24
NT = (((1,), (1,)), ((), ()))
BF = jnp.bfloat16
F32 = jnp.float32


def dot(left, right, dims=(((1,), (0,)), ((), ()))):
    return lax.dot_general(left, right, dims, preferred_element_type=F32)


def iota(shape, dim):
    return lax.broadcasted_iota(jnp.int32, shape, dim)


def roll(value, shift):
    width = value.shape[1]
    return pltpu.roll(value, shift % width, 1) if shift % width else value


def toeplitz(row, rows, shift=LANES - HALO):
    row = roll(row, shift % 8)
    return pltpu.roll(jnp.broadcast_to(row, (rows, row.shape[1])), shift // 8 * 8, 1, stride=1, stride_axis=0)


def lanczos(offset):
    return (
        3.0
        * jnp.sin(jnp.pi * offset)
        * jnp.sin(jnp.pi * offset / 3.0)
        / (jnp.pi * jnp.pi * offset * offset)
    )


def lanczos_weights(frac):
    shape = (8, frac.shape[1])
    shift = iota(shape, 0) - 2
    return lanczos(jnp.broadcast_to(frac, shape) - shift.astype(F32)).astype(BF).astype(F32)


def tile_kernel(
    coeff_hbm, weight_hbm, owner_hbm, block_hbm,
    tile_hbm, row_taps_hbm, col_taps_hbm, start_x_hbm, frac_x_hbm, start_y_hbm, frac_y_hbm,
    out_ref,
    coeff_ref, weight_ref, owner_ref, block_ref,
    tile_ref, row_taps_ref, col_taps_ref, start_x_ref, frac_x_ref, start_y_ref, frac_y_ref,
    sems, taps_ref, stack_ref, matched_ref, shifted_ref, col_ref, count_ref,
):
    pairs = [
        (row_taps_hbm, row_taps_ref), (tile_hbm, tile_ref), (col_taps_hbm, col_taps_ref),
        (coeff_hbm, coeff_ref), (frac_x_hbm, frac_x_ref), (start_x_hbm, start_x_ref),
        (start_y_hbm, start_y_ref), (frac_y_hbm, frac_y_ref), (weight_hbm, weight_ref),
        (owner_hbm, owner_ref), (block_hbm, block_ref),
    ]
    copies = [pltpu.make_async_copy(src, dst, sems.at[n]) for n, (src, dst) in enumerate(pairs)]
    for copy in copies:
        copy.start()
    taps_ref[...] = jnp.zeros_like(taps_ref)
    stack_ref[0:R, :] = jnp.zeros((R, LANES), BF)
    stack_ref[(SPT + 1) * R:(SPT + 2) * R, :] = jnp.zeros((R, LANES), BF)
    peers = out_ref.shape[0]
    for o in range(peers):
        count_ref[o] = 0
    out_ref[...] = jnp.zeros_like(out_ref)
    for copy in copies:
        copy.wait()
    taps_ref[0:NB, 0:KW] = row_taps_ref[...].astype(F32)
    taps_ref[8:8 + NB, 0:KW] = col_taps_ref[...].astype(F32)
    row_band = jnp.concatenate([toeplitz(taps_ref[k:k + 1, :], LANES) for k in range(NB)], axis=0).astype(BF)
    col_bands = [toeplitz(taps_ref[8 + k:9 + k, 0:LANES], R)[:, 0:R].astype(BF) for k in range(NB)]
    for s in range(SPT):
        stack_ref[(s + 1) * R:(s + 2) * R, :] = tile_ref[0, :, s * LANES:(s + 1) * LANES]
    group = 4
    width = group * LANES
    for g in range(SPT // group):
        first = g * group * R
        rows = group * R
        window = jnp.concatenate(
            [stack_ref[first + j * R:first + j * R + rows, :] for j in range(3)], axis=1
        )
        across = dot(window, row_band, NT).astype(BF)
        column = iota((1, width), 1) + g * width
        x_coord = (2 * column - (W - 1)).astype(F32) / (W - 1)
        y_coord = (2 * iota((R, 1), 0) - (R - 1)).astype(F32) / (R - 1)
        matched = jnp.zeros((R, width), F32)
        for k in range(NB):
            term = jnp.concatenate(
                [across[j * R:(j + 1) * R, k * LANES:(k + 1) * LANES] for j in range(group)], axis=1
            )
            basis_term = dot(col_bands[k], term)
            coeff_map = coeff_ref[0, 0, k] + coeff_ref[1, 0, k] * x_coord + coeff_ref[2, 0, k] * y_coord
            matched = matched + coeff_map * basis_term
        matched_ref[:, g * width:(g + 1) * width] = matched.astype(BF).astype(F32)
    for s in range(6):
        shifted_ref[s * R:(s + 1) * R, :] = roll(matched_ref[...], 2 - s).astype(BF)
    weights_x = lanczos_weights(frac_x_ref[...])
    chunk = 256
    for c in range(W // chunk):
        cols = slice(c * chunk, (c + 1) * chunk)
        chosen = (iota((W, chunk), 0) == start_x_ref[:, cols]).astype(F32).astype(BF)
        taken = dot(shifted_ref[...], chosen)
        total = weights_x[0:1, cols] * taken[0:R]
        for s in range(1, 6):
            total = total + weights_x[s:s + 1, cols] * taken[s * R:(s + 1) * R]
        col_ref[:, cols] = total.astype(BF)
    weights_y = lanczos_weights(frac_y_ref[...])
    step = iota((R, R), 0) - start_y_ref[...]
    warp_y = jnp.zeros((R, R), F32)
    for s in range(6):
        warp_y = jnp.where(step == s - 2, weights_y[s:s + 1, :], warp_y)
    warped = dot(warp_y.T.astype(BF), col_ref[...]).astype(BF)
    weight = weight_ref[...].astype(F32)
    row = iota((UNIT, LANES), 0)
    lane = iota((UNIT, LANES), 1)
    base = jnp.where((row == 2) & (lane < NOTE_LANES), weight, 0.0).astype(BF)
    for o in range(peers):
        out_ref[o, NOTE:NOTE + UNIT, :] = base

    def add_edges(owner, strip, lanes, at, count_lane):
        strip = strip.astype(F32)
        for t in range(2):
            piece = jnp.where(lane == count_lane, 1.0, 0.0) if t else jnp.zeros((UNIT, LANES), F32)
            for f in range(2):
                part = strip[(2 * t + f) * UNIT:(2 * t + f + 1) * UNIT]
                inside = (lane >= at[f]) & (lane < at[f] + HALO)
                piece = jnp.where(inside, roll(part, at[f] - lanes), piece)
            rows = slice(NOTE + t * UNIT, NOTE + (t + 1) * UNIT)
            out_ref[owner, rows, :] = (out_ref[owner, rows, :].astype(F32) + piece).astype(BF)

    for s in range(SPT):
        owner, block = owner_ref[0, s], block_ref[0, s]
        slot = count_ref[owner]
        count_ref[owner] = slot + 1
        strip = warped[:, s * LANES:(s + 1) * LANES]
        out_ref[owner, pl.ds(pl.multiple_of(slot * R, R), R), :] = strip
        note = jnp.where(row == 0, weight, jnp.where(row == 1, block.astype(F32), 0.0))
        note = jnp.where((lane // UNIT == slot) & (row < 2), note, 0.0)
        held = out_ref[owner, NOTE:NOTE + UNIT, :].astype(F32)
        out_ref[owner, NOTE:NOTE + UNIT, :] = (held + note).astype(BF)
        pl.when((block == SPT - 1) & (owner < peers - 1))(
            lambda: add_edges(owner + 1, strip, LANES - HALO, LEFT_AT, 0)
        )
        pl.when((block == 0) & (owner > 0))(lambda: add_edges(owner - 1, strip, 0, RIGHT_AT, 1))


def split(value):
    high = value.astype(BF)
    return high, (value - high.astype(F32)).astype(BF)


def taper_bands(width, rows, shift):
    lane = iota((1, width), 1)
    at = lane - HALO
    taps = jnp.where(lane < KW, 441 - at * at, 0).astype(F32)
    high, low = split(toeplitz(taps, rows, shift))
    return jnp.concatenate([high, low], axis=0)


def sum_kernel(in_ref, coadd_ref, mid_ref, chip_ref, next_ref, stack_ref):
    peers = in_ref.shape[0]
    depth = peers * NOTE_LANES
    notes = []
    per_row = LANES // NOTE_LANES
    lane = iota((UNIT, LANES), 1)
    for q in range(peers // per_row):
        total = jnp.zeros((UNIT, LANES), F32)
        for j in range(per_row):
            note = in_ref[q * per_row + j, NOTE:NOTE + UNIT, :].astype(F32)
            total = jnp.where(lane // NOTE_LANES == j, roll(note, j * NOTE_LANES), total)
        notes.append(total)
    notes = jnp.concatenate(notes, axis=1)
    weight, block, peer_weight = notes[0:1], notes[1:2], notes[2:3]
    same = iota((UNIT, depth), 0) == iota((UNIT, depth), 1) % UNIT
    spread = jnp.concatenate(
        [jnp.where(same, jnp.where(block == b, weight, 0.0), 0.0) for b in range(SPT)], axis=0
    ).astype(BF)
    parts = []
    for g in range(R // UNIT):
        pieces = [
            in_ref[v, slot * R + g * UNIT:slot * R + (g + 1) * UNIT, :]
            for v in range(peers) for slot in range(SLOTS)
        ]
        parts.append(jnp.concatenate(pieces, axis=0))
    parts.append(jnp.ones((depth, LANES), BF))
    total = dot(spread, jnp.concatenate(parts, axis=1))
    scale = 1.0 / (total[:, R // UNIT * LANES:] + 1.0)
    for b in range(SPT):
        for g in range(R // UNIT):
            rows = slice(b * UNIT, (b + 1) * UNIT)
            value = total[rows, g * LANES:(g + 1) * LANES] * scale[rows]
            coadd_ref[g * UNIT:(g + 1) * UNIT, b * LANES:(b + 1) * LANES] = value
            stack_ref[(b + 1) * R + g * UNIT:(b + 1) * R + (g + 1) * UNIT, :] = value
    same = iota((NOTE_LANES, depth), 0) == iota((NOTE_LANES, depth), 1) % NOTE_LANES
    edges = jnp.concatenate([in_ref[v, NOTE:MSG, :] for v in range(peers)], axis=0)
    edges = dot(jnp.where(same, peer_weight, 0.0).astype(BF), edges)
    for t in range(2):
        part = edges[t * UNIT:(t + 1) * UNIT]
        counts = edges[UNIT:2 * UNIT]
        left = part * (1.0 / (counts[:, 0:1] + 1.0))
        right = part * (1.0 / (counts[:, 1:2] + 1.0))
        for f in range(2):
            at = (2 * t + f) * UNIT
            stack_ref[at:at + UNIT, :] = roll(left, LANES - HALO - LEFT_AT[f])
            at += (SPT + 1) * R
            stack_ref[at:at + UNIT, :] = roll(right, -RIGHT_AT[f])
    band = taper_bands(3 * LANES, LANES, LANES - HALO)
    high, low = split(stack_ref[...])
    window = jnp.concatenate(
        [
            jnp.concatenate([part[j * R:(j + SPT) * R] for j in range(3)], axis=1)
            for part in (high, low)
        ],
        axis=0,
    )
    mid = dot(window, band, NT)
    mid = (mid[0:SPT * R] + mid[SPT * R:])
    mid = mid[:, 0:LANES] + mid[:, LANES:]
    for s in range(SPT):
        mid_ref[:, s * LANES:(s + 1) * LANES] = mid[s * R:(s + 1) * R]
    even = lax.axis_index("sky") % 2 == 0
    first, last = mid_ref[0:EDGE, :], mid_ref[R - EDGE:R, :]
    chip_ref[...] = jnp.where(even, last, first)
    next_ref[...] = jnp.where(even, first, last)


def down_kernel(mid_ref, chip_ref, next_ref, out_ref):
    norm = sum((1.0 - (a / 21.0) ** 2) ** 2 for a in range(-HALO, HALO + 1))
    even = lax.axis_index("sky") % 2 == 0
    chip, following = chip_ref[...], next_ref[...]
    above, below = jnp.where(even, following, chip), jnp.where(even, chip, following)
    rows = jnp.concatenate([above, mid_ref[...], below], axis=0)
    band = taper_bands(LANES, R, EDGE - HALO)[:, 0:R + 2 * EDGE]
    high, low = split(rows)
    total = dot(jnp.concatenate([band, band], axis=1), jnp.concatenate([high, low], axis=0))
    out_ref[...] = (total[0:R] + total[R:]) * (1.0 / (441.0 * 441.0 * norm))


def vmem(n):
    return [pl.BlockSpec(memory_space=pltpu.VMEM)] * n


GRANT = 56 * 1024 * 1024
PARAMS = pltpu.CompilerParams(vmem_limit_bytes=40 * 1024 * 1024)


def local(
    ccd_tiles, row_taps, col_taps, psf_coeffs, warp_start_x, warp_frac_x, warp_start_y, warp_frac_y,
    tile_weight, strip_owner, strip_block,
):
    peers = lax.axis_size("visit")
    operands = (
        psf_coeffs.transpose(2, 0, 1), tile_weight.reshape(1, 1), strip_owner.reshape(1, SPT), strip_block,
        ccd_tiles, row_taps, col_taps, warp_start_x, warp_frac_x, warp_start_y, warp_frac_y,
    )
    spaces = [pltpu.SMEM, pltpu.VMEM, pltpu.SMEM, pltpu.SMEM] + [pltpu.VMEM] * 7
    messages = pl.pallas_call(
        tile_kernel,
        out_shape=jax.ShapeDtypeStruct((peers, MSG, LANES), BF),
        in_specs=[pl.BlockSpec(memory_space=pltpu.HBM)] * len(operands),
        out_specs=pl.BlockSpec(memory_space=pltpu.VMEM),
        scratch_shapes=[space(x.shape, x.dtype) for space, x in zip(spaces, operands)] + [
            pltpu.SemaphoreType.DMA((len(operands),)),
            pltpu.VMEM((16, 3 * LANES), F32),
            pltpu.VMEM(((SPT + 2) * R, LANES), BF),
            pltpu.VMEM((R, W), F32),
            pltpu.VMEM((6 * R, W), BF),
            pltpu.VMEM((R, W), BF),
            pltpu.SMEM((peers,), jnp.int32),
        ],
        compiler_params=pltpu.CompilerParams(vmem_limit_bytes=GRANT),
    )(*operands)
    received = lax.all_to_all(messages, "visit", 0, 0, tiled=True)
    image = jax.ShapeDtypeStruct((R, W), F32)
    rows = jax.ShapeDtypeStruct((EDGE, W), F32)
    coadd, mid, to_chip, to_next = pl.pallas_call(
        sum_kernel,
        out_shape=(image, image, rows, rows),
        in_specs=vmem(1),
        out_specs=tuple(vmem(4)),
        scratch_shapes=[pltpu.VMEM(((SPT + 2) * R, LANES), F32)],
        compiler_params=PARAMS,
    )(received)
    size = lax.axis_size("sky")
    swap = lambda first: [p for i in range(first, size - 1, 2) for p in ((i, i + 1), (i + 1, i))]
    from_chip = lax.ppermute(to_chip, "sky", swap(0))
    from_next = lax.ppermute(to_next, "sky", swap(1))
    detection = pl.pallas_call(
        down_kernel,
        out_shape=image,
        in_specs=vmem(3),
        out_specs=pl.BlockSpec(memory_space=pltpu.VMEM),
        compiler_params=PARAMS,
    )(mid, from_chip, from_next)
    return coadd, detection


def solution(mesh):
    tiles = ("visit", "sky")
    in_specs = (
        P(tiles, None, None),
        P(),
        P(),
        P(tiles, None, None),
        P(tiles, None),
        P(tiles, None),
        P(tiles, None),
        P(tiles, None),
        P(tiles),
        P(tiles, None, None),
        P(tiles, None),
    )
    out_specs = (P("sky", "visit"), P("sky", "visit"))
    return jax.shard_map(local, mesh=mesh, in_specs=in_specs, out_specs=out_specs, check_vma=False)
```

time: 84.9 us -> 67.8 us (0.80)
  the two profiles are of different devices: /device:TPU:10 before, /device:TPU:1 now
where the time goes in v2:
time: 67.8 us; the launch traced here: 67.7 us
  blocking collectives  44.3 us (65%)
  Pallas kernels  11.5 us (17%)
  starting transfers between devices  6.66 us (10%)
  waiting for transfers between devices  3.93 us (6%)
  between operations  1.31 us (2%)
    all_to_all x1, blocking collectives, local(): received = lax.all_to_all(messages, 'visit', 0, 0, tiled=True)  44.3 us
    pallas_call x1, Pallas kernels, local(): pl.pallas_call(tile_kernel, out_shape=jax.ShapeDtypeStruct((peers, MSG, L...  8.62 us
    ppermute x1, waiting for transfers between devices, local(): from_next = lax.ppermute(to_next, 'sky', swap(1))  3.93 us
    ppermute x1, starting transfers between devices, local(): from_chip = lax.ppermute(to_chip, 'sky', swap(0))  3.62 us
    ppermute x1, starting transfers between devices, local(): from_next = lax.ppermute(to_next, 'sky', swap(1))  3.03 us
    pallas_call x1, Pallas kernels, local(): pl.pallas_call(sum_kernel, out_shape=(image, image, rows, rows), in_specs...  1.64 us
  transfers between devices with their start and end apart: 2, of which 1 were waited for; matrix products, arithmetic and copies ran while one was open for 0% of the time, Pallas kernels for 0%

profile of v2, /device:TPU:1, one launch (start us, length us, event | category | flops | bytes accessed | tf_op | source)
XLA Modules:
  0.0 67.7 jit_solution(12675532318475958506)
XLA Ops:
  1.3 8.6 %shard_map.122 = bf16[32,160,128]{2,1,0:T(8,128)(2,1)} custom-call(f32[3,1,5]{2,1,0:T(1,128)} %bitcast.4, bf16[1,1]{1,0:T(2,128)(2,1)} %bitcast.3.weight_hbm, s32[1,16]{1,0:T(1,128)} %bitcast.5, s32[1,16]{1,0:T(1,128)} %block_hbm.1, bf16[1,64,2048]{2,1,0:T(8,128)(2,1)} %tile_hbm.1, bf16[5,41]{1,0:T(8,128)(2,1)} %row_taps_hbm.1, bf16[5,41]{1,0:T(8,128)(2,1)} %col_taps_hbm.1, ...), custom_call_target="tpu_custom_call" | custom-call | tf_op jit(solution)/shard_map/pallas_call | solution.py:276
  9.9 44.3 %all_to_all.5.in_ref = bf16[32,160,128]{2,1,0:T(8,128)(2,1)S(1)} all-to-all(bf16[32,160,128]{2,1,0:T(8,128)(2,1)} %shard_map.122), channel_id=1, replica_groups=mesh['visit'=32,'sky'=8] {'visit'}, dimensions={0} | all-to-all | bytes 2621440 | tf_op jit(solution)/shard_map/all_to_all | solution.py:292
  54.2 1.6 %shard_map.123 = (f32[64,2048]{1,0:T(8,128)}, f32[64,2048]{1,0:T(8,128)S(1)}, f32[24,2048]{1,0:T(8,128)S(1)}, f32[24,2048]{1,0:T(8,128)S(1)}) custom-call(bf16[32,160,128]{2,1,0:T(8,128)(2,1)S(1)} %all_to_all.5.in_ref), custom_call_target="tpu_custom_call" | custom-call | tf_op jit(solution)/shard_map/pallas_call | solution.py:295
  55.8 3.6 %collective-permute-start = (f32[24,2048]{1,0:T(8,128)S(1)}, f32[24,2048]{1,0:T(8,128)S(1)}, u32[]{:S(2)}, u32[]{:S(2)}) collective-permute-start(f32[24,2048]{1,0:T(8,128)S(1)} %get-tuple-element.8), channel_id=1, source_target_pairs={{0,1},{1,0},{2,3},{3,2},{4,5},{5,4},{6,7},{7,6},{8,9},{9,8},{10,11... | collective-permute-start | bytes 589832 | tf_op jit(solution)/shard_map/ppermute | solution.py:305
  59.5 3.0 %collective-permute-start.1 = (f32[24,2048]{1,0:T(8,128)S(1)}, f32[24,2048]{1,0:T(8,128)S(1)}, u32[]{:S(2)}, u32[]{:S(2)}) collective-permute-start(f32[24,2048]{1,0:T(8,128)S(1)} %get-tuple-element.9), channel_id=1, source_target_pairs={{1,2},{2,1},{3,4},{4,3},{5,6},{6,5},{9,10},{10,9},{11,12},{12,11},... | collective-permute-start | bytes 589832 | tf_op jit(solution)/shard_map/ppermute | solution.py:306
  62.5 0.0 collective-permute-done.chip_ref
  62.5 3.9 %collective-permute-done.1.next_ref = f32[24,2048]{1,0:T(8,128)S(1)} collective-permute-done((f32[24,2048]{1,0:T(8,128)S(1)}, f32[24,2048]{1,0:T(8,128)S(1)}, u32[]{:S(2)}, u32[]{:S(2)}) %collective-permute-start.1) | collective-permute-done | bytes 196640 | tf_op jit(solution)/shard_map/ppermute | solution.py:306
  66.4 1.3 %shard_map.124 = f32[64,2048]{1,0:T(8,128)} custom-call(f32[64,2048]{1,0:T(8,128)S(1)} %get-tuple-element.7.mid_ref, f32[24,2048]{1,0:T(8,128)S(1)} %collective-permute-done.chip_ref, f32[24,2048]{1,0:T(8,128)S(1)} %collective-permute-done.1.next_ref), custom_call_target="tpu_custom_call" | custom-call | tf_op jit(solution)/shard_map/pallas_call | solution.py:307
Async XLA Ops:
  55.8 6.7 %collective-permute-start = (f32[24,2048]{1,0:T(8,128)S(1)}, f32[24,2048]{1,0:T(8,128)S(1)}, u32[]{:S(2)}, u32[]{:S(2)}) collective-permute-start(f32[24,2048]{1,0:T(8,128)S(1)} %get-tuple-element.8), channel_id=1, source_target_pairs={{0,1},{1,0},{2,3},{3,2},{4,5},{5,4},{6,7},{7,6},{8,9},{9,8},{10,11... | collective-permute-start | bytes 589832 | tf_op jit(solution)/shard_map/ppermute | solution.py:305
  59.5 7.0 %collective-permute-start.1 = (f32[24,2048]{1,0:T(8,128)S(1)}, f32[24,2048]{1,0:T(8,128)S(1)}, u32[]{:S(2)}, u32[]{:S(2)}) collective-permute-start(f32[24,2048]{1,0:T(8,128)S(1)} %get-tuple-element.9), channel_id=1, source_target_pairs={{1,2},{2,1},{3,4},{4,3},{5,6},{6,5},{9,10},{10,9},{11,12},{12,11},... | collective-permute-start | bytes 589832 | tf_op jit(solution)/shard_map/ppermute | solution.py:306

commit v3 on v2

--- a/solution.py
+++ b/solution.py
@@ -15,10 +15,12 @@
 LANES = 128
 UNIT = 16
 NOTE = SLOTS * R
-MSG = NOTE + 2 * UNIT
+AUX = 24
+MSG = NOTE + AUX
 NOTE_LANES = 2 * UNIT
-LEFT_AT = (32, 80)
-RIGHT_AT = (52, 100)
+PLACE = 2 * HALO
+NOTE_AT = 2 * PLACE
+COUNT_AT = 3 * PLACE
 EDGE = 24
 NT = (((1,), (1,)), ((), ()))
 BF = jnp.bfloat16
@@ -64,7 +66,7 @@
     out_ref,
     coeff_ref, weight_ref, owner_ref, block_ref,
     tile_ref, row_taps_ref, col_taps_ref, start_x_ref, frac_x_ref, start_y_ref, frac_y_ref,
-    sems, taps_ref, stack_ref, matched_ref, shifted_ref, col_ref, count_ref,
+    sems, taps_ref, window_ref, matched_ref, source_ref, col_ref, count_ref,
 ):
     pairs = [
         (row_taps_hbm, row_taps_ref), (tile_hbm, tile_ref), (col_taps_hbm, col_taps_ref),
@@ -76,8 +78,6 @@
     for copy in copies:
         copy.start()
     taps_ref[...] = jnp.zeros_like(taps_ref)
-    stack_ref[0:R, :] = jnp.zeros((R, LANES), BF)
-    stack_ref[(SPT + 1) * R:(SPT + 2) * R, :] = jnp.zeros((R, LANES), BF)
     peers = out_ref.shape[0]
     for o in range(peers):
         count_ref[o] = 0
@@ -86,18 +86,24 @@
         copy.wait()
     taps_ref[0:NB, 0:KW] = row_taps_ref[...].astype(F32)
     taps_ref[8:8 + NB, 0:KW] = col_taps_ref[...].astype(F32)
-    row_band = jnp.concatenate([toeplitz(taps_ref[k:k + 1, :], LANES) for k in range(NB)], axis=0).astype(BF)
+    row_band = jnp.concatenate([toeplitz(taps_ref[k:k + 1, :], LANES, 0) for k in range(NB)], axis=0).astype(BF)
     col_bands = [toeplitz(taps_ref[8 + k:9 + k, 0:LANES], R)[:, 0:R].astype(BF) for k in range(NB)]
-    for s in range(SPT):
-        stack_ref[(s + 1) * R:(s + 2) * R, :] = tile_ref[0, :, s * LANES:(s + 1) * LANES]
+    moved = roll(tile_ref[0].astype(F32), HALO)
+    before = iota((R, LANES), 1) < HALO
+    for s in range(SPT + 1):
+        strip = moved[:, s % SPT * LANES:(s % SPT + 1) * LANES]
+        if s % SPT == 0:
+            strip = jnp.where(before == (s > 0), strip, 0.0)
+        strip = strip.astype(BF)
+        if s < SPT:
+            window_ref[s * R:(s + 1) * R, 0:LANES] = strip
+        if s > 0:
+            window_ref[(s - 1) * R:s * R, LANES:] = strip
     group = 4
     width = group * LANES
     for g in range(SPT // group):
-        first = g * group * R
         rows = group * R
-        window = jnp.concatenate(
-            [stack_ref[first + j * R:first + j * R + rows, :] for j in range(3)], axis=1
-        )
+        window = window_ref[g * rows:(g + 1) * rows, :]
         across = dot(window, row_band, NT).astype(BF)
         column = iota((1, width), 1) + g * width
         x_coord = (2 * column - (W - 1)).astype(F32) / (W - 1)
@@ -111,17 +117,27 @@
             coeff_map = coeff_ref[0, 0, k] + coeff_ref[1, 0, k] * x_coord + coeff_ref[2, 0, k] * y_coord
             matched = matched + coeff_map * basis_term
         matched_ref[:, g * width:(g + 1) * width] = matched.astype(BF).astype(F32)
-    for s in range(6):
-        shifted_ref[s * R:(s + 1) * R, :] = roll(matched_ref[...], 2 - s).astype(BF)
+    moved = roll(matched_ref[...], 2)
+    for s in range(SPT):
+        strip = moved[:, s * LANES:(s + 1) * LANES].astype(BF)
+        source_ref[s * R:(s + 1) * R, 0:LANES] = strip
+        before = (s - 1) % SPT
+        source_ref[before * R:(before + 1) * R, LANES:] = strip
     weights_x = lanczos_weights(frac_x_ref[...])
     chunk = 256
+    deep = LANES + 8
     for c in range(W // chunk):
         cols = slice(c * chunk, (c + 1) * chunk)
-        chosen = (iota((W, chunk), 0) == start_x_ref[:, cols]).astype(F32).astype(BF)
-        taken = dot(shifted_ref[...], chosen)
-        total = weights_x[0:1, cols] * taken[0:R]
-        for s in range(1, 6):
-            total = total + weights_x[s:s + 1, cols] * taken[s * R:(s + 1) * R]
+        start = start_x_ref[:, cols]
+        tap = iota((deep, chunk), 0) - start % LANES
+        taps = jnp.zeros((deep, chunk), F32)
+        for s in range(6):
+            taps = jnp.where(tap == s, weights_x[s:s + 1, cols], taps)
+        taps = jnp.concatenate([taps, jnp.zeros((2 * LANES - deep, chunk), F32)], axis=0).astype(BF)
+        found = dot(source_ref[...], taps)
+        total = found[0:R]
+        for s in range(1, SPT):
+            total = jnp.where(start // LANES == s, found[s * R:(s + 1) * R], total)
         col_ref[:, cols] = total.astype(BF)
     weights_y = lanczos_weights(frac_y_ref[...])
     step = iota((R, R), 0) - start_y_ref[...]
@@ -130,22 +146,31 @@
         warp_y = jnp.where(step == s - 2, weights_y[s:s + 1, :], warp_y)
     warped = dot(warp_y.T.astype(BF), col_ref[...]).astype(BF)
     weight = weight_ref[...].astype(F32)
-    row = iota((UNIT, LANES), 0)
-    lane = iota((UNIT, LANES), 1)
-    base = jnp.where((row == 2) & (lane < NOTE_LANES), weight, 0.0).astype(BF)
+    row = iota((AUX, LANES), 0)
+    lane = iota((AUX, LANES), 1)
+    place = lane - NOTE_AT
+    last = row - (AUX - 8)
+    noted = (last >= 0) & (place >= 0) & (place < NOTE_LANES)
+    base = jnp.where(noted & (last == 2), weight, 0.0).astype(BF)
     for o in range(peers):
-        out_ref[o, NOTE:NOTE + UNIT, :] = base
-
-    def add_edges(owner, strip, lanes, at, count_lane):
+        out_ref[o, NOTE:MSG, :] = base
+
+    def add(owner, piece):
+        out_ref[owner, NOTE:MSG, :] = (out_ref[owner, NOTE:MSG, :].astype(F32) + piece).astype(BF)
+
+    def add_edges(owner, strip, lanes, side):
         strip = strip.astype(F32)
-        for t in range(2):
-            piece = jnp.where(lane == count_lane, 1.0, 0.0) if t else jnp.zeros((UNIT, LANES), F32)
-            for f in range(2):
-                part = strip[(2 * t + f) * UNIT:(2 * t + f + 1) * UNIT]
-                inside = (lane >= at[f]) & (lane < at[f] + HALO)
-                piece = jnp.where(inside, roll(part, at[f] - lanes), piece)
-            rows = slice(NOTE + t * UNIT, NOTE + (t + 1) * UNIT)
-            out_ref[owner, rows, :] = (out_ref[owner, rows, :].astype(F32) + piece).astype(BF)
+        units = []
+        for t in range(AUX // 8):
+            at = lane[0:8] - side * HALO
+            unit = jnp.where(lane[0:8] == COUNT_AT + side, 1.0, 0.0)
+            for f in range(3):
+                n = 3 * t + f
+                if n < R // 8:
+                    part = roll(strip[n * 8:(n + 1) * 8], f * PLACE + side * HALO - lanes)
+                    unit = jnp.where((at >= f * PLACE) & (at < f * PLACE + HALO), part, unit)
+            units.append(unit)
+        add(owner, jnp.concatenate(units, axis=0))
 
     for s in range(SPT):
         owner, block = owner_ref[0, s], block_ref[0, s]
@@ -153,14 +178,12 @@
         count_ref[owner] = slot + 1
         strip = warped[:, s * LANES:(s + 1) * LANES]
         out_ref[owner, pl.ds(pl.multiple_of(slot * R, R), R), :] = strip
-        note = jnp.where(row == 0, weight, jnp.where(row == 1, block.astype(F32), 0.0))
-        note = jnp.where((lane // UNIT == slot) & (row < 2), note, 0.0)
-        held = out_ref[owner, NOTE:NOTE + UNIT, :].astype(F32)
-        out_ref[owner, NOTE:NOTE + UNIT, :] = (held + note).astype(BF)
+        note = jnp.where(last == 0, weight, jnp.where(last == 1, block.astype(F32), 0.0))
+        add(owner, jnp.where(noted & (place // UNIT == slot), note, 0.0))
         pl.when((block == SPT - 1) & (owner < peers - 1))(
-            lambda: add_edges(owner + 1, strip, LANES - HALO, LEFT_AT, 0)
+            lambda: add_edges(owner + 1, strip, LANES - HALO, 0)
         )
-        pl.when((block == 0) & (owner > 0))(lambda: add_edges(owner - 1, strip, 0, RIGHT_AT, 1))
+        pl.when((block == 0) & (owner > 0))(lambda: add_edges(owner - 1, strip, 0, 1))
 
 
 def split(value):
@@ -179,14 +202,15 @@
 def sum_kernel(in_ref, coadd_ref, mid_ref, chip_ref, next_ref, stack_ref):
     peers = in_ref.shape[0]
     depth = peers * NOTE_LANES
+    aux = [in_ref[v, NOTE:MSG, :].astype(F32) for v in range(peers)]
     notes = []
     per_row = LANES // NOTE_LANES
-    lane = iota((UNIT, LANES), 1)
+    lane = iota((8, LANES), 1)
     for q in range(peers // per_row):
-        total = jnp.zeros((UNIT, LANES), F32)
+        total = jnp.zeros((8, LANES), F32)
         for j in range(per_row):
-            note = in_ref[q * per_row + j, NOTE:NOTE + UNIT, :].astype(F32)
-            total = jnp.where(lane // NOTE_LANES == j, roll(note, j * NOTE_LANES), total)
+            note = roll(aux[q * per_row + j][AUX - 8:], j * NOTE_LANES - NOTE_AT)
+            total = jnp.where(lane // NOTE_LANES == j, note, total)
         notes.append(total)
     notes = jnp.concatenate(notes, axis=1)
     weight, block, peer_weight = notes[0:1], notes[1:2], notes[2:3]
@@ -210,19 +234,17 @@
             value = total[rows, g * LANES:(g + 1) * LANES] * scale[rows]
             coadd_ref[g * UNIT:(g + 1) * UNIT, b * LANES:(b + 1) * LANES] = value
             stack_ref[(b + 1) * R + g * UNIT:(b + 1) * R + (g + 1) * UNIT, :] = value
-    same = iota((NOTE_LANES, depth), 0) == iota((NOTE_LANES, depth), 1) % NOTE_LANES
-    edges = jnp.concatenate([in_ref[v, NOTE:MSG, :] for v in range(peers)], axis=0)
+    same = iota((AUX, depth), 0) == iota((AUX, depth), 1) % NOTE_LANES
+    gap = jnp.zeros((NOTE_LANES - AUX, LANES), F32)
+    edges = jnp.concatenate([x for v in range(peers) for x in (aux[v], gap)], axis=0).astype(BF)
     edges = dot(jnp.where(same, peer_weight, 0.0).astype(BF), edges)
-    for t in range(2):
-        part = edges[t * UNIT:(t + 1) * UNIT]
-        counts = edges[UNIT:2 * UNIT]
-        left = part * (1.0 / (counts[:, 0:1] + 1.0))
-        right = part * (1.0 / (counts[:, 1:2] + 1.0))
-        for f in range(2):
-            at = (2 * t + f) * UNIT
-            stack_ref[at:at + UNIT, :] = roll(left, LANES - HALO - LEFT_AT[f])
-            at += (SPT + 1) * R
-            stack_ref[at:at + UNIT, :] = roll(right, -RIGHT_AT[f])
+    for side, block in enumerate((0, SPT + 1)):
+        sum_weight = edges[AUX - 8:AUX - 7, COUNT_AT + side:COUNT_AT + side + 1]
+        value = edges * (1.0 / (sum_weight + 1.0))
+        for n in range(R // 8):
+            t, f = n // 3, n % 3
+            to = (LANES - HALO, 0)[side] - f * PLACE - side * HALO
+            stack_ref[block * R + n * 8:block * R + n * 8 + 8, :] = roll(value[t * 8:t * 8 + 8], to)
     band = taper_bands(3 * LANES, LANES, LANES - HALO)
     high, low = split(stack_ref[...])
     window = jnp.concatenate(
@@ -263,6 +285,26 @@
 PARAMS = pltpu.CompilerParams(vmem_limit_bytes=40 * 1024 * 1024)
 
 
+def tile_call(peers, *operands):
+    spaces = [pltpu.SMEM, pltpu.VMEM, pltpu.SMEM, pltpu.SMEM] + [pltpu.VMEM] * 7
+    return pl.pallas_call(
+        tile_kernel,
+        out_shape=jax.ShapeDtypeStruct((peers, MSG, LANES), BF),
+        in_specs=[pl.BlockSpec(memory_space=pltpu.HBM)] * len(operands),
+        out_specs=pl.BlockSpec(memory_space=pltpu.VMEM),
+        scratch_shapes=[space(x.shape, x.dtype) for space, x in zip(spaces, operands)] + [
+            pltpu.SemaphoreType.DMA((len(operands),)),
+            pltpu.VMEM((16, 2 * LANES), F32),
+            pltpu.VMEM((SPT * R, 2 * LANES), BF),
+            pltpu.VMEM((R, W), F32),
+            pltpu.VMEM((SPT * R, 2 * LANES), BF),
+            pltpu.VMEM((R, W), BF),
+            pltpu.SMEM((peers,), jnp.int32),
+        ],
+        compiler_params=pltpu.CompilerParams(vmem_limit_bytes=GRANT),
+    )(*operands)
+
+
 def local(
     ccd_tiles, row_taps, col_taps, psf_coeffs, warp_start_x, warp_frac_x, warp_start_y, warp_frac_y,
     tile_weight, strip_owner, strip_block,
@@ -272,23 +314,7 @@
         psf_coeffs.transpose(2, 0, 1), tile_weight.reshape(1, 1), strip_owner.reshape(1, SPT), strip_block,
         ccd_tiles, row_taps, col_taps, warp_start_x, warp_frac_x, warp_start_y, warp_frac_y,
     )
-    spaces = [pltpu.SMEM, pltpu.VMEM, pltpu.SMEM, pltpu.SMEM] + [pltpu.VMEM] * 7
-    messages = pl.pallas_call(
-        tile_kernel,
-        out_shape=jax.ShapeDtypeStruct((peers, MSG, LANES), BF),
-        in_specs=[pl.BlockSpec(memory_space=pltpu.HBM)] * len(operands),
-        out_specs=pl.BlockSpec(memory_space=pltpu.VMEM),
-        scratch_shapes=[space(x.shape, x.dtype) for space, x in zip(spaces, operands)] + [
-            pltpu.SemaphoreType.DMA((len(operands),)),
-            pltpu.VMEM((16, 3 * LANES), F32),
-            pltpu.VMEM(((SPT + 2) * R, LANES), BF),
-            pltpu.VMEM((R, W), F32),
-            pltpu.VMEM((6 * R, W), BF),
-            pltpu.VMEM((R, W), BF),
-            pltpu.SMEM((peers,), jnp.int32),
-        ],
-        compiler_params=pltpu.CompilerParams(vmem_limit_bytes=GRANT),
-    )(*operands)
+    messages = tile_call(peers, *operands)
     received = lax.all_to_all(messages, "visit", 0, 0, tiled=True)
     image = jax.ShapeDtypeStruct((R, W), F32)
     rows = jax.ShapeDtypeStruct((EDGE, W), F32)
@@ -302,8 +328,8 @@
     )(received)
     size = lax.axis_size("sky")
     swap = lambda first: [p for i in range(first, size - 1, 2) for p in ((i, i + 1), (i + 1, i))]
+    from_next = lax.ppermute(to_next, "sky", swap(1))
     from_chip = lax.ppermute(to_chip, "sky", swap(0))
-    from_next = lax.ppermute(to_next, "sky", swap(1))
     detection = pl.pallas_call(
         down_kernel,
         out_shape=image,

time: 67.8 us -> 64.5 us (0.951)
  Pallas kernels: 11.5 us -> 9.13 us
  blocking collectives: 44.3 us -> 43.6 us
    pallas_call x1, Pallas kernels: 8.62 us -> 6.16 us  [tile_call(): pl.pallas_call(tile_kernel, out_shape=jax.ShapeDtypeStruct((peers, MSG, L...]
    all_to_all x1, blocking collectives: 44.3 us -> 43.6 us  [local(): received = lax.all_to_all(messages, 'visit', 0, 0, tiled=True)]
where the time goes in v3:
time: 64.5 us; the launch traced here: 64.2 us
  blocking collectives  43.6 us (68%)
  Pallas kernels  9.13 us (14%)
  starting transfers between devices  6.44 us (10%)
  waiting for transfers between devices  3.74 us (6%)
  between operations  1.31 us (2%)
    all_to_all x1, blocking collectives, local(): received = lax.all_to_all(messages, 'visit', 0, 0, tiled=True)  43.6 us
    pallas_call x1, Pallas kernels, tile_call(): pl.pallas_call(tile_kernel, out_shape=jax.ShapeDtypeStruct((peers, MSG, L...  6.16 us
    ppermute x1, waiting for transfers between devices, local(): from_next = lax.ppermute(to_next, 'sky', swap(1))  3.74 us
    ppermute x1, starting transfers between devices, local(): from_chip = lax.ppermute(to_chip, 'sky', swap(0))  3.23 us
    ppermute x1, starting transfers between devices, local(): from_next = lax.ppermute(to_next, 'sky', swap(1))  3.22 us
    pallas_call x1, Pallas kernels, local(): pl.pallas_call(sum_kernel, out_shape=(image, image, rows, rows), in_specs...  1.69 us
  transfers between devices with their start and end apart: 2, of which 1 were waited for; matrix products, arithmetic and copies ran while one was open for 0% of the time, Pallas kernels for 0%

profile of v3, /device:TPU:1, one launch (start us, length us, event | category | flops | bytes accessed | tf_op | source)
XLA Modules:
  0.0 64.2 jit_solution(5243644394232863179)
XLA Ops:
  1.3 6.2 %shard_map.122 = bf16[32,152,128]{2,1,0:T(8,128)(2,1)} custom-call(f32[3,1,5]{2,1,0:T(1,128)} %bitcast.4, bf16[1,1]{1,0:T(2,128)(2,1)} %bitcast.3.weight_hbm, s32[1,16]{1,0:T(1,128)} %bitcast.5, s32[1,16]{1,0:T(1,128)} %block_hbm.1, bf16[1,64,2048]{2,1,0:T(8,128)(2,1)} %tile_hbm.1, bf16[5,41]{1,0:T(8,128)(2,1)} %row_taps_hbm.1, bf16[5,41]{1,0:T(8,128)(2,1)} %col_taps_hbm.1, ...), custom_call_target="tpu_custom_call" | custom-call | tf_op jit(solution)/shard_map/pallas_call | solution.py:290
  7.5 43.6 %all_to_all.5.in_ref = bf16[32,152,128]{2,1,0:T(8,128)(2,1)S(1)} all-to-all(bf16[32,152,128]{2,1,0:T(8,128)(2,1)} %shard_map.122), channel_id=1, replica_groups=mesh['visit'=32,'sky'=8] {'visit'}, dimensions={0} | all-to-all | bytes 2490368 | tf_op jit(solution)/shard_map/all_to_all | solution.py:318
  51.0 1.7 %shard_map.123 = (f32[64,2048]{1,0:T(8,128)}, f32[64,2048]{1,0:T(8,128)S(1)}, f32[24,2048]{1,0:T(8,128)S(1)}, f32[24,2048]{1,0:T(8,128)S(1)}) custom-call(bf16[32,152,128]{2,1,0:T(8,128)(2,1)S(1)} %all_to_all.5.in_ref), custom_call_target="tpu_custom_call" | custom-call | tf_op jit(solution)/shard_map/pallas_call | solution.py:321
  52.7 3.2 %collective-permute-start = (f32[24,2048]{1,0:T(8,128)S(1)}, f32[24,2048]{1,0:T(8,128)S(1)}, u32[]{:S(2)}, u32[]{:S(2)}) collective-permute-start(f32[24,2048]{1,0:T(8,128)S(1)} %get-tuple-element.8), channel_id=1, source_target_pairs={{0,1},{1,0},{2,3},{3,2},{4,5},{5,4},{6,7},{7,6},{8,9},{9,8},{10,11... | collective-permute-start | bytes 589832 | tf_op jit(solution)/shard_map/ppermute | solution.py:332
  56.0 3.2 %collective-permute-start.1 = (f32[24,2048]{1,0:T(8,128)S(1)}, f32[24,2048]{1,0:T(8,128)S(1)}, u32[]{:S(2)}, u32[]{:S(2)}) collective-permute-start(f32[24,2048]{1,0:T(8,128)S(1)} %get-tuple-element.9), channel_id=1, source_target_pairs={{1,2},{2,1},{3,4},{4,3},{5,6},{6,5},{9,10},{10,9},{11,12},{12,11},... | collective-permute-start | bytes 589832 | tf_op jit(solution)/shard_map/ppermute | solution.py:331
  59.2 0.0 collective-permute-done.chip_ref
  59.2 3.7 %collective-permute-done.1.next_ref = f32[24,2048]{1,0:T(8,128)S(1)} collective-permute-done((f32[24,2048]{1,0:T(8,128)S(1)}, f32[24,2048]{1,0:T(8,128)S(1)}, u32[]{:S(2)}, u32[]{:S(2)}) %collective-permute-start.1) | collective-permute-done | bytes 196640 | tf_op jit(solution)/shard_map/ppermute | solution.py:331
  62.9 1.3 %shard_map.124 = f32[64,2048]{1,0:T(8,128)} custom-call(f32[64,2048]{1,0:T(8,128)S(1)} %get-tuple-element.7.mid_ref, f32[24,2048]{1,0:T(8,128)S(1)} %collective-permute-done.chip_ref, f32[24,2048]{1,0:T(8,128)S(1)} %collective-permute-done.1.next_ref), custom_call_target="tpu_custom_call" | custom-call | tf_op jit(solution)/shard_map/pallas_call | solution.py:333
Async XLA Ops:
  52.7 6.5 %collective-permute-start = (f32[24,2048]{1,0:T(8,128)S(1)}, f32[24,2048]{1,0:T(8,128)S(1)}, u32[]{:S(2)}, u32[]{:S(2)}) collective-permute-start(f32[24,2048]{1,0:T(8,128)S(1)} %get-tuple-element.8), channel_id=1, source_target_pairs={{0,1},{1,0},{2,3},{3,2},{4,5},{5,4},{6,7},{7,6},{8,9},{9,8},{10,11... | collective-permute-start | bytes 589832 | tf_op jit(solution)/shard_map/ppermute | solution.py:332
  56.0 7.0 %collective-permute-start.1 = (f32[24,2048]{1,0:T(8,128)S(1)}, f32[24,2048]{1,0:T(8,128)S(1)}, u32[]{:S(2)}, u32[]{:S(2)}) collective-permute-start(f32[24,2048]{1,0:T(8,128)S(1)} %get-tuple-element.9), channel_id=1, source_target_pairs={{1,2},{2,1},{3,4},{4,3},{5,6},{6,5},{9,10},{10,9},{11,12},{12,11},... | collective-permute-start | bytes 589832 | tf_op jit(solution)/shard_map/ppermute | solution.py:331

commit v4 on v3

--- a/solution.py
+++ b/solution.py
@@ -45,19 +45,24 @@
     return pltpu.roll(jnp.broadcast_to(row, (rows, row.shape[1])), shift // 8 * 8, 1, stride=1, stride_axis=0)
 
 
-def lanczos(offset):
-    return (
-        3.0
-        * jnp.sin(jnp.pi * offset)
-        * jnp.sin(jnp.pi * offset / 3.0)
-        / (jnp.pi * jnp.pi * offset * offset)
-    )
+def sin_pi(value):
+    folded = jnp.where(value > 0.5, 1.0 - value, jnp.where(value < -0.5, -1.0 - value, value))
+    angle = jnp.pi * folded
+    square = angle * angle
+    total = jnp.full_like(angle, -1.0 / 39916800.0)
+    for term in (1.0 / 362880.0, -1.0 / 5040.0, 1.0 / 120.0, -1.0 / 6.0, 1.0):
+        total = total * square + term
+    return total * angle
 
 
 def lanczos_weights(frac):
     shape = (8, frac.shape[1])
-    shift = iota(shape, 0) - 2
-    return lanczos(jnp.broadcast_to(frac, shape) - shift.astype(F32)).astype(BF).astype(F32)
+    shift = iota(shape, 0)
+    offset = jnp.broadcast_to(frac, shape) - (shift - 2).astype(F32)
+    sine = sin_pi(jnp.broadcast_to(frac, shape))
+    sine = jnp.where(shift % 2 == 0, sine, -sine)
+    weights = 3.0 * sine * sin_pi(offset * (1.0 / 3.0)) / (jnp.pi * jnp.pi * offset * offset)
+    return weights.astype(BF).astype(F32)
 
 
 def tile_kernel(
@@ -99,7 +104,7 @@
             window_ref[s * R:(s + 1) * R, 0:LANES] = strip
         if s > 0:
             window_ref[(s - 1) * R:s * R, LANES:] = strip
-    group = 4
+    group = 16
     width = group * LANES
     for g in range(SPT // group):
         rows = group * R
@@ -124,21 +129,24 @@
         before = (s - 1) % SPT
         source_ref[before * R:(before + 1) * R, LANES:] = strip
     weights_x = lanczos_weights(frac_x_ref[...])
-    chunk = 256
-    deep = LANES + 8
+    chunk = 512
+    deep = LANES + 16
+    order = iota((deep, chunk), 0).astype(F32).astype(BF)
     for c in range(W // chunk):
         cols = slice(c * chunk, (c + 1) * chunk)
         start = start_x_ref[:, cols]
-        tap = iota((deep, chunk), 0) - start % LANES
-        taps = jnp.zeros((deep, chunk), F32)
+        tap = order - (start % LANES).astype(F32).astype(BF)
+        taps = jnp.zeros((deep, chunk), BF)
         for s in range(6):
-            taps = jnp.where(tap == s, weights_x[s:s + 1, cols], taps)
-        taps = jnp.concatenate([taps, jnp.zeros((2 * LANES - deep, chunk), F32)], axis=0).astype(BF)
+            taps = jnp.where(tap == s, weights_x[s:s + 1, cols].astype(BF), taps)
+        taps = jnp.concatenate([taps, jnp.zeros((2 * LANES - deep, chunk), BF)], axis=0)
         found = dot(source_ref[...], taps)
-        total = found[0:R]
+        place = jnp.broadcast_to(start // LANES, (8, chunk))
+        total = found[0:R].reshape(R // 8, 8, chunk)
         for s in range(1, SPT):
-            total = jnp.where(start // LANES == s, found[s * R:(s + 1) * R], total)
-        col_ref[:, cols] = total.astype(BF)
+            part = found[s * R:(s + 1) * R].reshape(R // 8, 8, chunk)
+            total = jnp.where((place == s)[None], part, total)
+        col_ref[:, cols] = total.reshape(R, chunk).astype(BF)
     weights_y = lanczos_weights(frac_y_ref[...])
     step = iota((R, R), 0) - start_y_ref[...]
     warp_y = jnp.zeros((R, R), F32)
@@ -180,10 +188,13 @@
         out_ref[owner, pl.ds(pl.multiple_of(slot * R, R), R), :] = strip
         note = jnp.where(last == 0, weight, jnp.where(last == 1, block.astype(F32), 0.0))
         add(owner, jnp.where(noted & (place // UNIT == slot), note, 0.0))
-        pl.when((block == SPT - 1) & (owner < peers - 1))(
-            lambda: add_edges(owner + 1, strip, LANES - HALO, 0)
-        )
-        pl.when((block == 0) & (owner > 0))(lambda: add_edges(owner - 1, strip, 0, 1))
+
+        @pl.when((block == SPT - 1) | (block == 0))
+        def _():
+            pl.when((block > 0) & (owner < peers - 1))(
+                lambda: add_edges(owner + 1, strip, LANES - HALO, 0)
+            )
+            pl.when((block == 0) & (owner > 0))(lambda: add_edges(owner - 1, strip, 0, 1))
 
 
 def split(value):
@@ -261,14 +272,14 @@
         mid_ref[:, s * LANES:(s + 1) * LANES] = mid[s * R:(s + 1) * R]
     even = lax.axis_index("sky") % 2 == 0
     first, last = mid_ref[0:EDGE, :], mid_ref[R - EDGE:R, :]
-    chip_ref[...] = jnp.where(even, last, first)
-    next_ref[...] = jnp.where(even, first, last)
+    chip_ref[...] = jnp.where(even, last, first).astype(BF)
+    next_ref[...] = jnp.where(even, first, last).astype(BF)
 
 
 def down_kernel(mid_ref, chip_ref, next_ref, out_ref):
     norm = sum((1.0 - (a / 21.0) ** 2) ** 2 for a in range(-HALO, HALO + 1))
     even = lax.axis_index("sky") % 2 == 0
-    chip, following = chip_ref[...], next_ref[...]
+    chip, following = chip_ref[...].astype(F32), next_ref[...].astype(F32)
     above, below = jnp.where(even, following, chip), jnp.where(even, chip, following)
     rows = jnp.concatenate([above, mid_ref[...], below], axis=0)
     band = taper_bands(LANES, R, EDGE - HALO)[:, 0:R + 2 * EDGE]
@@ -305,6 +316,29 @@
     )(*operands)
 
 
+def sum_call(received):
+    image = jax.ShapeDtypeStruct((R, W), F32)
+    rows = jax.ShapeDtypeStruct((EDGE, W), BF)
+    return pl.pallas_call(
+        sum_kernel,
+        out_shape=(image, image, rows, rows),
+        in_specs=vmem(1),
+        out_specs=tuple(vmem(4)),
+        scratch_shapes=[pltpu.VMEM(((SPT + 2) * R, LANES), F32)],
+        compiler_params=PARAMS,
+    )(received)
+
+
+def down_call(mid, from_chip, from_next):
+    return pl.pallas_call(
+        down_kernel,
+        out_shape=jax.ShapeDtypeStruct((R, W), F32),
+        in_specs=vmem(3),
+        out_specs=pl.BlockSpec(memory_space=pltpu.VMEM),
+        compiler_params=PARAMS,
+    )(mid, from_chip, from_next)
+
+
 def local(
     ccd_tiles, row_taps, col_taps, psf_coeffs, warp_start_x, warp_frac_x, warp_start_y, warp_frac_y,
     tile_weight, strip_owner, strip_block,
@@ -316,27 +350,12 @@
     )
     messages = tile_call(peers, *operands)
     received = lax.all_to_all(messages, "visit", 0, 0, tiled=True)
-    image = jax.ShapeDtypeStruct((R, W), F32)
-    rows = jax.ShapeDtypeStruct((EDGE, W), F32)
-    coadd, mid, to_chip, to_next = pl.pallas_call(
-        sum_kernel,
-        out_shape=(image, image, rows, rows),
-        in_specs=vmem(1),
-        out_specs=tuple(vmem(4)),
-        scratch_shapes=[pltpu.VMEM(((SPT + 2) * R, LANES), F32)],
-        compiler_params=PARAMS,
-    )(received)
+    coadd, mid, to_chip, to_next = sum_call(received)
     size = lax.axis_size("sky")
     swap = lambda first: [p for i in range(first, size - 1, 2) for p in ((i, i + 1), (i + 1, i))]
     from_next = lax.ppermute(to_next, "sky", swap(1))
     from_chip = lax.ppermute(to_chip, "sky", swap(0))
-    detection = pl.pallas_call(
-        down_kernel,
-        out_shape=image,
-        in_specs=vmem(3),
-        out_specs=pl.BlockSpec(memory_space=pltpu.VMEM),
-        compiler_params=PARAMS,
-    )(mid, from_chip, from_next)
+    detection = down_call(mid, from_chip, from_next)
     return coadd, detection
 
 

time: 64.5 us -> 62.3 us (0.966)
  Pallas kernels: 9.13 us -> 7.85 us
  waiting for transfers between devices: 3.74 us -> 2.73 us
    pallas_call x1, Pallas kernels: 6.16 us -> 5.04 us  [tile_call(): pl.pallas_call(tile_kernel, out_shape=jax.ShapeDtypeStruct((peers, MSG, L...]
    ppermute x1, waiting for transfers between devices: 3.74 us -> 2.73 us  [local(): from_next = lax.ppermute(to_next, 'sky', swap(1))]
where the time goes in v4:
time: 62.3 us; the launch traced here: 62.1 us
  blocking collectives  43.7 us (70%)
  Pallas kernels  7.85 us (13%)
  starting transfers between devices  6.49 us (10%)
  waiting for transfers between devices  2.73 us (4%)
  between operations  1.32 us (2%)
    all_to_all x1, blocking collectives, local(): received = lax.all_to_all(messages, 'visit', 0, 0, tiled=True)  43.7 us
    pallas_call x1, Pallas kernels, tile_call(): pl.pallas_call(tile_kernel, out_shape=jax.ShapeDtypeStruct((peers, MSG, L...  5.04 us
    ppermute x1, starting transfers between devices, local(): from_chip = lax.ppermute(to_chip, 'sky', swap(0))  3.31 us
    ppermute x1, starting transfers between devices, local(): from_next = lax.ppermute(to_next, 'sky', swap(1))  3.18 us
    ppermute x1, waiting for transfers between devices, local(): from_next = lax.ppermute(to_next, 'sky', swap(1))  2.73 us
    pallas_call x1, Pallas kernels, sum_call(): pl.pallas_call(sum_kernel, out_shape=(image, image, rows, rows), in_specs...  1.53 us
    pallas_call x1, Pallas kernels, down_call(): pl.pallas_call(down_kernel, out_shape=jax.ShapeDtypeStruct((R, W), F32),...  1.28 us
  transfers between devices with their start and end apart: 2, of which 1 were waited for; matrix products, arithmetic and copies ran while one was open for 0% of the time, Pallas kernels for 0%

profile of v4, /device:TPU:1, one launch (start us, length us, event | category | flops | bytes accessed | tf_op | source)
XLA Modules:
  0.0 62.1 jit_solution(9260042248923919707)
XLA Ops:
  1.3 5.0 %shard_map.122 = bf16[32,152,128]{2,1,0:T(8,128)(2,1)} custom-call(f32[3,1,5]{2,1,0:T(1,128)} %bitcast.4, bf16[1,1]{1,0:T(2,128)(2,1)} %bitcast.3.weight_hbm, s32[1,16]{1,0:T(1,128)} %bitcast.5, s32[1,16]{1,0:T(1,128)} %block_hbm.1, bf16[1,64,2048]{2,1,0:T(8,128)(2,1)} %tile_hbm.1, bf16[5,41]{1,0:T(8,128)(2,1)} %row_taps_hbm.1, bf16[5,41]{1,0:T(8,128)(2,1)} %col_taps_hbm.1, ...), custom_call_target="tpu_custom_call" | custom-call | tf_op jit(solution)/shard_map/pallas_call | solution.py:301
  6.3 43.7 %all_to_all.5.in_ref = bf16[32,152,128]{2,1,0:T(8,128)(2,1)S(1)} all-to-all(bf16[32,152,128]{2,1,0:T(8,128)(2,1)} %shard_map.122), channel_id=1, replica_groups=mesh['visit'=32,'sky'=8] {'visit'}, dimensions={0} | all-to-all | bytes 2490368 | tf_op jit(solution)/shard_map/all_to_all | solution.py:352
  50.1 1.5 %shard_map.123 = (f32[64,2048]{1,0:T(8,128)}, f32[64,2048]{1,0:T(8,128)S(1)}, bf16[24,2048]{1,0:T(8,128)(2,1)S(1)}, bf16[24,2048]{1,0:T(8,128)(2,1)S(1)}) custom-call(bf16[32,152,128]{2,1,0:T(8,128)(2,1)S(1)} %all_to_all.5.in_ref), custom_call_target="tpu_custom_call" | custom-call | tf_op jit(solution)/shard_map/pallas_call | solution.py:322
  51.6 3.3 %collective-permute-start = (bf16[24,2048]{1,0:T(8,128)(2,1)S(1)}, bf16[24,2048]{1,0:T(8,128)(2,1)S(1)}, u32[]{:S(2)}, u32[]{:S(2)}) collective-permute-start(bf16[24,2048]{1,0:T(8,128)(2,1)S(1)} %get-tuple-element.8), channel_id=1, source_target_pairs={{0,1},{1,0},{2,3},{3,2},{4,5},{5,4},{6,7},{7,6},{8,9},{9,8},{10,11... | collective-permute-start | bytes 294920 | tf_op jit(solution)/shard_map/ppermute | solution.py:357
  54.9 3.2 %collective-permute-start.1 = (bf16[24,2048]{1,0:T(8,128)(2,1)S(1)}, bf16[24,2048]{1,0:T(8,128)(2,1)S(1)}, u32[]{:S(2)}, u32[]{:S(2)}) collective-permute-start(bf16[24,2048]{1,0:T(8,128)(2,1)S(1)} %get-tuple-element.9), channel_id=1, source_target_pairs={{1,2},{2,1},{3,4},{4,3},{5,6},{6,5},{9,10},{10,9},{11,12},{12,11},... | collective-permute-start | bytes 294920 | tf_op jit(solution)/shard_map/ppermute | solution.py:356
  58.1 0.0 collective-permute-done.chip_ref
  58.1 2.7 %collective-permute-done.1.next_ref = bf16[24,2048]{1,0:T(8,128)(2,1)S(1)} collective-permute-done((bf16[24,2048]{1,0:T(8,128)(2,1)S(1)}, bf16[24,2048]{1,0:T(8,128)(2,1)S(1)}, u32[]{:S(2)}, u32[]{:S(2)}) %collective-permute-start.1) | collective-permute-done | bytes 98336 | tf_op jit(solution)/shard_map/ppermute | solution.py:356
  60.8 1.3 %shard_map.124 = f32[64,2048]{1,0:T(8,128)} custom-call(f32[64,2048]{1,0:T(8,128)S(1)} %get-tuple-element.7.mid_ref, bf16[24,2048]{1,0:T(8,128)(2,1)S(1)} %collective-permute-done.chip_ref, bf16[24,2048]{1,0:T(8,128)(2,1)S(1)} %collective-permute-done.1.next_ref), custom_call_target="tpu_custom_call" | custom-call | tf_op jit(solution)/shard_map/pallas_call | solution.py:333
Async XLA Ops:
  51.6 6.5 %collective-permute-start = (bf16[24,2048]{1,0:T(8,128)(2,1)S(1)}, bf16[24,2048]{1,0:T(8,128)(2,1)S(1)}, u32[]{:S(2)}, u32[]{:S(2)}) collective-permute-start(bf16[24,2048]{1,0:T(8,128)(2,1)S(1)} %get-tuple-element.8), channel_id=1, source_target_pairs={{0,1},{1,0},{2,3},{3,2},{4,5},{5,4},{6,7},{7,6},{8,9},{9,8},{10,11... | collective-permute-start | bytes 294920 | tf_op jit(solution)/shard_map/ppermute | solution.py:357
  54.9 5.9 %collective-permute-start.1 = (bf16[24,2048]{1,0:T(8,128)(2,1)S(1)}, bf16[24,2048]{1,0:T(8,128)(2,1)S(1)}, u32[]{:S(2)}, u32[]{:S(2)}) collective-permute-start(bf16[24,2048]{1,0:T(8,128)(2,1)S(1)} %get-tuple-element.9), channel_id=1, source_target_pairs={{1,2},{2,1},{3,4},{4,3},{5,6},{6,5},{9,10},{10,9},{11,12},{12,11},... | collective-permute-start | bytes 294920 | tf_op jit(solution)/shard_map/ppermute | solution.py:356

commit v5 on v4

--- a/solution.py
+++ b/solution.py
@@ -210,7 +210,12 @@
     return jnp.concatenate([high, low], axis=0)
 
 
-def sum_kernel(in_ref, coadd_ref, mid_ref, chip_ref, next_ref, stack_ref):
+def band_kernel(across_ref, down_ref):
+    across_ref[...] = taper_bands(3 * LANES, LANES, LANES - HALO)
+    down_ref[...] = taper_bands(LANES, R, EDGE - HALO)
+
+
+def sum_kernel(in_ref, band_ref, coadd_ref, mid_ref, chip_ref, next_ref, stack_ref):
     peers = in_ref.shape[0]
     depth = peers * NOTE_LANES
     aux = [in_ref[v, NOTE:MSG, :].astype(F32) for v in range(peers)]
@@ -256,7 +261,7 @@
             t, f = n // 3, n % 3
             to = (LANES - HALO, 0)[side] - f * PLACE - side * HALO
             stack_ref[block * R + n * 8:block * R + n * 8 + 8, :] = roll(value[t * 8:t * 8 + 8], to)
-    band = taper_bands(3 * LANES, LANES, LANES - HALO)
+    band = band_ref[...]
     high, low = split(stack_ref[...])
     window = jnp.concatenate(
         [
@@ -276,13 +281,13 @@
     next_ref[...] = jnp.where(even, first, last).astype(BF)
 
 
-def down_kernel(mid_ref, chip_ref, next_ref, out_ref):
+def down_kernel(mid_ref, chip_ref, next_ref, band_ref, out_ref):
     norm = sum((1.0 - (a / 21.0) ** 2) ** 2 for a in range(-HALO, HALO + 1))
     even = lax.axis_index("sky") % 2 == 0
     chip, following = chip_ref[...].astype(F32), next_ref[...].astype(F32)
     above, below = jnp.where(even, following, chip), jnp.where(even, chip, following)
     rows = jnp.concatenate([above, mid_ref[...], below], axis=0)
-    band = taper_bands(LANES, R, EDGE - HALO)[:, 0:R + 2 * EDGE]
+    band = band_ref[:, 0:R + 2 * EDGE]
     high, low = split(rows)
     total = dot(jnp.concatenate([band, band], axis=1), jnp.concatenate([high, low], axis=0))
     out_ref[...] = (total[0:R] + total[R:]) * (1.0 / (441.0 * 441.0 * norm))
@@ -316,27 +321,27 @@
     )(*operands)
 
 
-def sum_call(received):
+def sum_call(received, band):
     image = jax.ShapeDtypeStruct((R, W), F32)
     rows = jax.ShapeDtypeStruct((EDGE, W), BF)
     return pl.pallas_call(
         sum_kernel,
         out_shape=(image, image, rows, rows),
-        in_specs=vmem(1),
+        in_specs=vmem(2),
         out_specs=tuple(vmem(4)),
         scratch_shapes=[pltpu.VMEM(((SPT + 2) * R, LANES), F32)],
         compiler_params=PARAMS,
-    )(received)
-
-
-def down_call(mid, from_chip, from_next):
+    )(received, band)
+
+
+def down_call(mid, from_chip, from_next, band):
     return pl.pallas_call(
         down_kernel,
         out_shape=jax.ShapeDtypeStruct((R, W), F32),
-        in_specs=vmem(3),
+        in_specs=vmem(4),
         out_specs=pl.BlockSpec(memory_space=pltpu.VMEM),
         compiler_params=PARAMS,
-    )(mid, from_chip, from_next)
+    )(mid, from_chip, from_next, band)
 
 
 def local(
@@ -349,13 +354,19 @@
         ccd_tiles, row_taps, col_taps, warp_start_x, warp_frac_x, warp_start_y, warp_frac_y,
     )
     messages = tile_call(peers, *operands)
+    band_across, band_down = pl.pallas_call(
+        band_kernel,
+        out_shape=(jax.ShapeDtypeStruct((2 * LANES, 3 * LANES), BF), jax.ShapeDtypeStruct((2 * R, LANES), BF)),
+        out_specs=tuple(vmem(2)),
+        compiler_params=PARAMS,
+    )()
     received = lax.all_to_all(messages, "visit", 0, 0, tiled=True)
-    coadd, mid, to_chip, to_next = sum_call(received)
+    coadd, mid, to_chip, to_next = sum_call(received, band_across)
     size = lax.axis_size("sky")
     swap = lambda first: [p for i in range(first, size - 1, 2) for p in ((i, i + 1), (i + 1, i))]
     from_next = lax.ppermute(to_next, "sky", swap(1))
     from_chip = lax.ppermute(to_chip, "sky", swap(0))
-    detection = down_call(mid, from_chip, from_next)
+    detection = down_call(mid, from_chip, from_next, band_down)
     return coadd, detection
 
 

time: 62.3 us -> 61 us (0.979)
  blocking collectives: 43.7 us -> 0 us
  waiting for transfers between devices: 2.73 us -> 30.6 us
  starting transfers between devices: 6.49 us -> 20.5 us
    all_to_all x1 -> x0, blocking collectives: 43.7 us -> none  [local(): received = lax.all_to_all(messages, 'visit', 0, 0, tiled=True)]
    all_to_all x0 -> x1, waiting for transfers between devices: none -> 28.2 us  [local(): received = lax.all_to_all(messages, 'visit', 0, 0, tiled=True)]
    all_to_all x0 -> x1, starting transfers between devices: none -> 11.6 us  [local(): received = lax.all_to_all(messages, 'visit', 0, 0, tiled=True)]
    ppermute x1, starting transfers between devices: 3.31 us -> 5.34 us  [local(): from_chip = lax.ppermute(to_chip, 'sky', swap(0))]
  transfers between devices with their start and end apart: 2 -> 3, of which waited for: 1 -> 2; matrix products, arithmetic and copies ran while one was open for 0% -> 0% of each run, Pallas kernels for 0% -> 0%
where the time goes in v5:
time: 61 us; the launch traced here: 60.6 us
  waiting for transfers between devices  30.6 us (50%)
  starting transfers between devices  20.5 us (34%)
  Pallas kernels  8.2 us (13%)
  between operations  1.33 us (2%)
    all_to_all x1, waiting for transfers between devices, local(): received = lax.all_to_all(messages, 'visit', 0, 0, tiled=True)  28.2 us
    all_to_all x1, starting transfers between devices, local(): received = lax.all_to_all(messages, 'visit', 0, 0, tiled=True)  11.6 us
    ppermute x1, starting transfers between devices, local(): from_chip = lax.ppermute(to_chip, 'sky', swap(0))  5.34 us
    pallas_call x1, Pallas kernels, tile_call(): pl.pallas_call(tile_kernel, out_shape=jax.ShapeDtypeStruct((peers, MSG, L...  5.33 us
    ppermute x1, starting transfers between devices, local(): from_next = lax.ppermute(to_next, 'sky', swap(1))  3.52 us
    ppermute x1, waiting for transfers between devices, local(): from_next = lax.ppermute(to_next, 'sky', swap(1))  2.38 us
    pallas_call x1, Pallas kernels, sum_call(): pl.pallas_call(sum_kernel, out_shape=(image, image, rows, rows), in_specs...  1.54 us
  transfers between devices with their start and end apart: 3, of which 2 were waited for; matrix products, arithmetic and copies ran while one was open for 0% of the time, Pallas kernels for 0%

profile of v5, /device:TPU:1, one launch (start us, length us, event | category | flops | bytes accessed | tf_op | source)
XLA Modules:
  0.0 60.6 jit_solution(14270040793116753598)
XLA Ops:
  1.3 5.3 %shard_map.122 = bf16[32,152,128]{2,1,0:T(8,128)(2,1)} custom-call(f32[3,1,5]{2,1,0:T(1,128)} %bitcast.4, bf16[1,1]{1,0:T(2,128)(2,1)} %bitcast.3.weight_hbm, s32[1,16]{1,0:T(1,128)} %bitcast.5, s32[1,16]{1,0:T(1,128)} %block_hbm.1, bf16[1,64,2048]{2,1,0:T(8,128)(2,1)} %tile_hbm.1, bf16[5,41]{1,0:T(8,128)(2,1)} %row_taps_hbm.1, bf16[5,41]{1,0:T(8,128)(2,1)} %col_taps_hbm.1, ...), custom_call_target="tpu_custom_call" | custom-call | tf_op jit(solution)/shard_map/pallas_call | solution.py:306
  6.6 11.6 %all-to-all-start = ((bf16[32,152,128]{2,1,0:T(8,128)(2,1)}), bf16[32,152,128]{2,1,0:T(8,128)(2,1)S(1)}, u32[]{:S(2)}, u32[]{:S(2)}) async-start(bf16[32,152,128]{2,1,0:T(8,128)(2,1)} %shard_map.122), calls=%async_computation | async-start | bytes 2490368 | tf_op jit(solution)/shard_map/all_to_all | solution.py:363
  18.2 0.2 shard_map.123
  18.4 28.2 %all-to-all-done.in_ref = bf16[32,152,128]{2,1,0:T(8,128)(2,1)S(1)} async-done(((bf16[32,152,128]{2,1,0:T(8,128)(2,1)}), bf16[32,152,128]{2,1,0:T(8,128)(2,1)S(1)}, u32[]{:S(2)}, u32[]{:S(2)}) %all-to-all-start) | async-done | bytes 1245216 | tf_op jit(solution)/shard_map/all_to_all | solution.py:363
  46.7 1.5 %shard_map.124 = (f32[64,2048]{1,0:T(8,128)}, f32[64,2048]{1,0:T(8,128)S(1)}, bf16[24,2048]{1,0:T(8,128)(2,1)S(1)}, bf16[24,2048]{1,0:T(8,128)(2,1)S(1)}) custom-call(bf16[32,152,128]{2,1,0:T(8,128)(2,1)S(1)} %all-to-all-done.in_ref, bf16[256,384]{1,0:T(8,128)(2,1)S(1)} %get-tuple-element.8.band_ref), custom_call_target="tpu_custom_call" | custom-call | tf_op jit(solution)/shard_map/pallas_call | solution.py:327
  48.2 5.3 %collective-permute-start = (bf16[24,2048]{1,0:T(8,128)(2,1)S(1)}, bf16[24,2048]{1,0:T(8,128)(2,1)S(1)}, u32[]{:S(2)}, u32[]{:S(2)}) collective-permute-start(bf16[24,2048]{1,0:T(8,128)(2,1)S(1)} %get-tuple-element.11), channel_id=1, source_target_pairs={{0,1},{1,0},{2,3},{3,2},{4,5},{5,4},{6,7},{7,6},{8,9},{9,8},{10,11... | collective-permute-start | bytes 294920 | tf_op jit(solution)/shard_map/ppermute | solution.py:368
  53.5 3.5 %collective-permute-start.1 = (bf16[24,2048]{1,0:T(8,128)(2,1)S(1)}, bf16[24,2048]{1,0:T(8,128)(2,1)S(1)}, u32[]{:S(2)}, u32[]{:S(2)}) collective-permute-start(bf16[24,2048]{1,0:T(8,128)(2,1)S(1)} %get-tuple-element.12), channel_id=1, source_target_pairs={{1,2},{2,1},{3,4},{4,3},{5,6},{6,5},{9,10},{10,9},{11,12},{12,11},... | collective-permute-start | bytes 294920 | tf_op jit(solution)/shard_map/ppermute | solution.py:367
  57.1 0.0 collective-permute-done.chip_ref
  57.1 2.4 %collective-permute-done.1.next_ref = bf16[24,2048]{1,0:T(8,128)(2,1)S(1)} collective-permute-done((bf16[24,2048]{1,0:T(8,128)(2,1)S(1)}, bf16[24,2048]{1,0:T(8,128)(2,1)S(1)}, u32[]{:S(2)}, u32[]{:S(2)}) %collective-permute-start.1) | collective-permute-done | bytes 98336 | tf_op jit(solution)/shard_map/ppermute | solution.py:367
  59.5 1.1 %shard_map.125 = f32[64,2048]{1,0:T(8,128)} custom-call(f32[64,2048]{1,0:T(8,128)S(1)} %get-tuple-element.10.mid_ref, bf16[24,2048]{1,0:T(8,128)(2,1)S(1)} %collective-permute-done.chip_ref, bf16[24,2048]{1,0:T(8,128)(2,1)S(1)} %collective-permute-done.1.next_ref, bf16[128,128]{1,0:T(8,128)(2,1)S(1)} %get-tuple-element.13.band_ref), custom_call_target="tpu_custom_call" | custom-call | tf_op jit(solution)/shard_map/pallas_call | solution.py:338
Async XLA Ops:
  6.6 40.0 %all-to-all-start = ((bf16[32,152,128]{2,1,0:T(8,128)(2,1)}), bf16[32,152,128]{2,1,0:T(8,128)(2,1)S(1)}, u32[]{:S(2)}, u32[]{:S(2)}) async-start(bf16[32,152,128]{2,1,0:T(8,128)(2,1)} %shard_map.122), calls=%async_computation | async-start | bytes 2490368 | tf_op jit(solution)/shard_map/all_to_all | solution.py:363
  48.2 8.9 %collective-permute-start = (bf16[24,2048]{1,0:T(8,128)(2,1)S(1)}, bf16[24,2048]{1,0:T(8,128)(2,1)S(1)}, u32[]{:S(2)}, u32[]{:S(2)}) collective-permute-start(bf16[24,2048]{1,0:T(8,128)(2,1)S(1)} %get-tuple-element.11), channel_id=1, source_target_pairs={{0,1},{1,0},{2,3},{3,2},{4,5},{5,4},{6,7},{7,6},{8,9},{9,8},{10,11... | collective-permute-start | bytes 294920 | tf_op jit(solution)/shard_map/ppermute | solution.py:368
  53.5 5.9 %collective-permute-start.1 = (bf16[24,2048]{1,0:T(8,128)(2,1)S(1)}, bf16[24,2048]{1,0:T(8,128)(2,1)S(1)}, u32[]{:S(2)}, u32[]{:S(2)}) collective-permute-start(bf16[24,2048]{1,0:T(8,128)(2,1)S(1)} %get-tuple-element.12), channel_id=1, source_target_pairs={{1,2},{2,1},{3,4},{4,3},{5,6},{6,5},{9,10},{10,9},{11,12},{12,11},... | collective-permute-start | bytes 294920 | tf_op jit(solution)/shard_map/ppermute | solution.py:367

commit v6 on v5

--- a/solution.py
+++ b/solution.py
@@ -63,6 +63,10 @@
     sine = jnp.where(shift % 2 == 0, sine, -sine)
     weights = 3.0 * sine * sin_pi(offset * (1.0 / 3.0)) / (jnp.pi * jnp.pi * offset * offset)
     return weights.astype(BF).astype(F32)
+
+
+def seat(o):
+    return (o + 2) % 8 * 4 + (o // 8 + 1) % 4
 
 
 def tile_kernel(
@@ -164,6 +168,7 @@
         out_ref[o, NOTE:MSG, :] = base
 
     def add(owner, piece):
+        owner = seat(owner)
         out_ref[owner, NOTE:MSG, :] = (out_ref[owner, NOTE:MSG, :].astype(F32) + piece).astype(BF)
 
     def add_edges(owner, strip, lanes, side):
@@ -185,7 +190,7 @@
         slot = count_ref[owner]
         count_ref[owner] = slot + 1
         strip = warped[:, s * LANES:(s + 1) * LANES]
-        out_ref[owner, pl.ds(pl.multiple_of(slot * R, R), R), :] = strip
+        out_ref[seat(owner), pl.ds(pl.multiple_of(slot * R, R), R), :] = strip
         note = jnp.where(last == 0, weight, jnp.where(last == 1, block.astype(F32), 0.0))
         add(owner, jnp.where(noted & (place // UNIT == slot), note, 0.0))
 
@@ -360,7 +365,8 @@
         out_specs=tuple(vmem(2)),
         compiler_params=PARAMS,
     )()
-    received = lax.all_to_all(messages, "visit", 0, 0, tiled=True)
+    groups = [sorted(range(peers), key=seat)]
+    received = lax.all_to_all(messages, "visit", 0, 0, tiled=True, axis_index_groups=groups)
     coadd, mid, to_chip, to_next = sum_call(received, band_across)
     size = lax.axis_size("sky")
     swap = lambda first: [p for i in range(first, size - 1, 2) for p in ((i, i + 1), (i + 1, i))]

time: 61 us -> 57.4 us (0.941)
  starting transfers between devices: 20.5 us -> 17.6 us
    ppermute x1, starting transfers between devices: 5.34 us -> 1.52 us  [local(): from_chip = lax.ppermute(to_chip, 'sky', swap(0))]
    all_to_all x1, starting transfers between devices: 11.6 us -> 12.8 us  [local(): lax.all_to_all(messages, 'visit', 0, 0, tiled=True, axis_index_groups=gro...]
    all_to_all x1, waiting for transfers between devices: 28.2 us -> 27.4 us  [local(): lax.all_to_all(messages, 'visit', 0, 0, tiled=True, axis_index_groups=gro...]
where the time goes in v6:
time: 57.4 us; the launch traced here: 57 us
  waiting for transfers between devices  30 us (52%)
  starting transfers between devices  17.6 us (31%)
  Pallas kernels  8.07 us (14%)
  between operations  1.33 us (2%)
    all_to_all x1, waiting for transfers between devices, local(): lax.all_to_all(messages, 'visit', 0, 0, tiled=True, axis_index_groups=gro...  27.4 us
    all_to_all x1, starting transfers between devices, local(): lax.all_to_all(messages, 'visit', 0, 0, tiled=True, axis_index_groups=gro...  12.8 us
    pallas_call x1, Pallas kernels, tile_call(): pl.pallas_call(tile_kernel, out_shape=jax.ShapeDtypeStruct((peers, MSG, L...  5.19 us
    ppermute x1, starting transfers between devices, local(): from_next = lax.ppermute(to_next, 'sky', swap(1))  3.34 us
    ppermute x1, waiting for transfers between devices, local(): from_next = lax.ppermute(to_next, 'sky', swap(1))  2.57 us
    pallas_call x1, Pallas kernels, sum_call(): pl.pallas_call(sum_kernel, out_shape=(image, image, rows, rows), in_specs...  1.54 us
    ppermute x1, starting transfers between devices, local(): from_chip = lax.ppermute(to_chip, 'sky', swap(0))  1.52 us
  transfers between devices with their start and end apart: 3, of which 2 were waited for; matrix products, arithmetic and copies ran while one was open for 0% of the time, Pallas kernels for 0%

profile of v6, /device:TPU:1, one launch (start us, length us, event | category | flops | bytes accessed | tf_op | source)
XLA Modules:
  0.0 57.0 jit_solution(12526250613790817602)
XLA Ops:
  1.3 5.2 %shard_map.122 = bf16[32,152,128]{2,1,0:T(8,128)(2,1)} custom-call(f32[3,1,5]{2,1,0:T(1,128)} %bitcast.4, bf16[1,1]{1,0:T(2,128)(2,1)} %bitcast.3.weight_hbm, s32[1,16]{1,0:T(1,128)} %bitcast.5, s32[1,16]{1,0:T(1,128)} %block_hbm.1, bf16[1,64,2048]{2,1,0:T(8,128)(2,1)} %tile_hbm.1, bf16[5,41]{1,0:T(8,128)(2,1)} %row_taps_hbm.1, bf16[5,41]{1,0:T(8,128)(2,1)} %col_taps_hbm.1, ...), custom_call_target="tpu_custom_call" | custom-call | tf_op jit(solution)/shard_map/pallas_call | solution.py:311
  6.5 12.8 %all-to-all-start = ((bf16[32,152,128]{2,1,0:T(8,128)(2,1)}), bf16[32,152,128]{2,1,0:T(8,128)(2,1)S(1)}, u32[]{:S(2)}, u32[]{:S(2)}) async-start(bf16[32,152,128]{2,1,0:T(8,128)(2,1)} %shard_map.122), calls=%async_computation | async-start | bytes 2490368 | tf_op jit(solution)/shard_map/all_to_all | solution.py:369
  19.3 0.2 shard_map.123
  19.5 27.4 %all-to-all-done.in_ref = bf16[32,152,128]{2,1,0:T(8,128)(2,1)S(1)} async-done(((bf16[32,152,128]{2,1,0:T(8,128)(2,1)}), bf16[32,152,128]{2,1,0:T(8,128)(2,1)S(1)}, u32[]{:S(2)}, u32[]{:S(2)}) %all-to-all-start) | async-done | bytes 1245216 | tf_op jit(solution)/shard_map/all_to_all | solution.py:369
  46.9 1.5 %shard_map.124 = (f32[64,2048]{1,0:T(8,128)}, f32[64,2048]{1,0:T(8,128)S(1)}, bf16[24,2048]{1,0:T(8,128)(2,1)S(1)}, bf16[24,2048]{1,0:T(8,128)(2,1)S(1)}) custom-call(bf16[32,152,128]{2,1,0:T(8,128)(2,1)S(1)} %all-to-all-done.in_ref, bf16[256,384]{1,0:T(8,128)(2,1)S(1)} %get-tuple-element.8.band_ref), custom_call_target="tpu_custom_call" | custom-call | tf_op jit(solution)/shard_map/pallas_call | solution.py:332
  48.4 1.5 %collective-permute-start = (bf16[24,2048]{1,0:T(8,128)(2,1)S(1)}, bf16[24,2048]{1,0:T(8,128)(2,1)S(1)}, u32[]{:S(2)}, u32[]{:S(2)}) collective-permute-start(bf16[24,2048]{1,0:T(8,128)(2,1)S(1)} %get-tuple-element.11), channel_id=1, source_target_pairs={{0,1},{1,0},{2,3},{3,2},{4,5},{5,4},{6,7},{7,6},{8,9},{9,8},{10,11... | collective-permute-start | bytes 294920 | tf_op jit(solution)/shard_map/ppermute | solution.py:374
  50.0 3.3 %collective-permute-start.1 = (bf16[24,2048]{1,0:T(8,128)(2,1)S(1)}, bf16[24,2048]{1,0:T(8,128)(2,1)S(1)}, u32[]{:S(2)}, u32[]{:S(2)}) collective-permute-start(bf16[24,2048]{1,0:T(8,128)(2,1)S(1)} %get-tuple-element.12), channel_id=1, source_target_pairs={{1,2},{2,1},{3,4},{4,3},{5,6},{6,5},{9,10},{10,9},{11,12},{12,11},... | collective-permute-start | bytes 294920 | tf_op jit(solution)/shard_map/ppermute | solution.py:373
  53.3 0.0 collective-permute-done.chip_ref
  53.3 2.6 %collective-permute-done.1.next_ref = bf16[24,2048]{1,0:T(8,128)(2,1)S(1)} collective-permute-done((bf16[24,2048]{1,0:T(8,128)(2,1)S(1)}, bf16[24,2048]{1,0:T(8,128)(2,1)S(1)}, u32[]{:S(2)}, u32[]{:S(2)}) %collective-permute-start.1) | collective-permute-done | bytes 98336 | tf_op jit(solution)/shard_map/ppermute | solution.py:373
  55.9 1.1 %shard_map.125 = f32[64,2048]{1,0:T(8,128)} custom-call(f32[64,2048]{1,0:T(8,128)S(1)} %get-tuple-element.10.mid_ref, bf16[24,2048]{1,0:T(8,128)(2,1)S(1)} %collective-permute-done.chip_ref, bf16[24,2048]{1,0:T(8,128)(2,1)S(1)} %collective-permute-done.1.next_ref, bf16[128,128]{1,0:T(8,128)(2,1)S(1)} %get-tuple-element.13.band_ref), custom_call_target="tpu_custom_call" | custom-call | tf_op jit(solution)/shard_map/pallas_call | solution.py:343
Async XLA Ops:
  6.5 40.4 %all-to-all-start = ((bf16[32,152,128]{2,1,0:T(8,128)(2,1)}), bf16[32,152,128]{2,1,0:T(8,128)(2,1)S(1)}, u32[]{:S(2)}, u32[]{:S(2)}) async-start(bf16[32,152,128]{2,1,0:T(8,128)(2,1)} %shard_map.122), calls=%async_computation | async-start | bytes 2490368 | tf_op jit(solution)/shard_map/all_to_all | solution.py:369
  48.4 4.9 %collective-permute-start = (bf16[24,2048]{1,0:T(8,128)(2,1)S(1)}, bf16[24,2048]{1,0:T(8,128)(2,1)S(1)}, u32[]{:S(2)}, u32[]{:S(2)}) collective-permute-start(bf16[24,2048]{1,0:T(8,128)(2,1)S(1)} %get-tuple-element.11), channel_id=1, source_target_pairs={{0,1},{1,0},{2,3},{3,2},{4,5},{5,4},{6,7},{7,6},{8,9},{9,8},{10,11... | collective-permute-start | bytes 294920 | tf_op jit(solution)/shard_map/ppermute | solution.py:374
  50.0 5.9 %collective-permute-start.1 = (bf16[24,2048]{1,0:T(8,128)(2,1)S(1)}, bf16[24,2048]{1,0:T(8,128)(2,1)S(1)}, u32[]{:S(2)}, u32[]{:S(2)}) collective-permute-start(bf16[24,2048]{1,0:T(8,128)(2,1)S(1)} %get-tuple-element.12), channel_id=1, source_target_pairs={{1,2},{2,1},{3,4},{4,3},{5,6},{6,5},{9,10},{10,9},{11,12},{12,11},... | collective-permute-start | bytes 294920 | tf_op jit(solution)/shard_map/ppermute | solution.py:373

commit v7 on v6

--- a/solution.py
+++ b/solution.py
@@ -11,6 +11,8 @@
 KW = 41
 HALO = 20
 SPT = 16
+SPAN = 240
+WINDOWS = -(-W // SPAN)
 SLOTS = 2
 LANES = 128
 UNIT = 16
@@ -126,28 +128,26 @@
             coeff_map = coeff_ref[0, 0, k] + coeff_ref[1, 0, k] * x_coord + coeff_ref[2, 0, k] * y_coord
             matched = matched + coeff_map * basis_term
         matched_ref[:, g * width:(g + 1) * width] = matched.astype(BF).astype(F32)
-    moved = roll(matched_ref[...], 2)
-    for s in range(SPT):
-        strip = moved[:, s * LANES:(s + 1) * LANES].astype(BF)
-        source_ref[s * R:(s + 1) * R, 0:LANES] = strip
-        before = (s - 1) % SPT
-        source_ref[before * R:(before + 1) * R, LANES:] = strip
+    for n in range(WINDOWS):
+        first = n * SPAN - 2
+        blocks = [(first // LANES + j) % SPT * LANES for j in range(3)]
+        region = jnp.concatenate([matched_ref[:, at:at + LANES] for at in blocks], axis=1)
+        source_ref[n * R:(n + 1) * R, :] = roll(region, -(first % LANES))[:, 0:2 * LANES].astype(BF)
     weights_x = lanczos_weights(frac_x_ref[...])
-    chunk = 512
-    deep = LANES + 16
-    order = iota((deep, chunk), 0).astype(F32).astype(BF)
+    chunk = 1024
+    order = iota((2 * LANES, chunk), 0).astype(F32).astype(BF)
     for c in range(W // chunk):
         cols = slice(c * chunk, (c + 1) * chunk)
         start = start_x_ref[:, cols]
-        tap = order - (start % LANES).astype(F32).astype(BF)
-        taps = jnp.zeros((deep, chunk), BF)
+        place = ((start.astype(F32) + 0.5) * (1.0 / SPAN)).astype(jnp.int32)
+        tap = order - (start - place * SPAN).astype(F32).astype(BF)
+        taps = jnp.zeros((2 * LANES, chunk), BF)
         for s in range(6):
             taps = jnp.where(tap == s, weights_x[s:s + 1, cols].astype(BF), taps)
-        taps = jnp.concatenate([taps, jnp.zeros((2 * LANES - deep, chunk), BF)], axis=0)
         found = dot(source_ref[...], taps)
-        place = jnp.broadcast_to(start // LANES, (8, chunk))
+        place = jnp.broadcast_to(place, (8, chunk))
         total = found[0:R].reshape(R // 8, 8, chunk)
-        for s in range(1, SPT):
+        for s in range(1, WINDOWS):
             part = found[s * R:(s + 1) * R].reshape(R // 8, 8, chunk)
             total = jnp.where((place == s)[None], part, total)
         col_ref[:, cols] = total.reshape(R, chunk).astype(BF)
@@ -216,7 +216,7 @@
 
 
 def band_kernel(across_ref, down_ref):
-    across_ref[...] = taper_bands(3 * LANES, LANES, LANES - HALO)
+    across_ref[...] = taper_bands(2 * LANES, LANES, 0)
     down_ref[...] = taper_bands(LANES, R, EDGE - HALO)
 
 
@@ -267,13 +267,11 @@
             to = (LANES - HALO, 0)[side] - f * PLACE - side * HALO
             stack_ref[block * R + n * 8:block * R + n * 8 + 8, :] = roll(value[t * 8:t * 8 + 8], to)
     band = band_ref[...]
-    high, low = split(stack_ref[...])
+    moved = roll(stack_ref[...], HALO)
+    strips = (SPT + 1) * R
+    moved = jnp.where(iota((strips, LANES), 1) < HALO, moved[0:strips], moved[R:])
     window = jnp.concatenate(
-        [
-            jnp.concatenate([part[j * R:(j + SPT) * R] for j in range(3)], axis=1)
-            for part in (high, low)
-        ],
-        axis=0,
+        [jnp.concatenate([part[0:SPT * R], part[R:]], axis=1) for part in split(moved)], axis=0
     )
     mid = dot(window, band, NT)
     mid = (mid[0:SPT * R] + mid[SPT * R:])
@@ -318,7 +316,7 @@
             pltpu.VMEM((16, 2 * LANES), F32),
             pltpu.VMEM((SPT * R, 2 * LANES), BF),
             pltpu.VMEM((R, W), F32),
-            pltpu.VMEM((SPT * R, 2 * LANES), BF),
+            pltpu.VMEM((WINDOWS * R, 2 * LANES), BF),
             pltpu.VMEM((R, W), BF),
             pltpu.SMEM((peers,), jnp.int32),
         ],
@@ -361,7 +359,7 @@
     messages = tile_call(peers, *operands)
     band_across, band_down = pl.pallas_call(
         band_kernel,
-        out_shape=(jax.ShapeDtypeStruct((2 * LANES, 3 * LANES), BF), jax.ShapeDtypeStruct((2 * R, LANES), BF)),
+        out_shape=(jax.ShapeDtypeStruct((2 * LANES, 2 * LANES), BF), jax.ShapeDtypeStruct((2 * R, LANES), BF)),
         out_specs=tuple(vmem(2)),
         compiler_params=PARAMS,
     )()

time: 57.4 us -> 57.1 us (level)
  no operation moved by 1% of the time
where the time goes in v7:
time: 57.1 us; the launch traced here: 56.9 us
  waiting for transfers between devices  30.4 us (53%)
  starting transfers between devices  17.2 us (30%)
  Pallas kernels  8.08 us (14%)
  between operations  1.32 us (2%)
    all_to_all x1, waiting for transfers between devices, local(): lax.all_to_all(messages, 'visit', 0, 0, tiled=True, axis_index_groups=gro...  27.5 us
    all_to_all x1, starting transfers between devices, local(): lax.all_to_all(messages, 'visit', 0, 0, tiled=True, axis_index_groups=gro...  12.6 us
    pallas_call x1, Pallas kernels, tile_call(): pl.pallas_call(tile_kernel, out_shape=jax.ShapeDtypeStruct((peers, MSG, L...  5.21 us
    ppermute x1, starting transfers between devices, local(): from_next = lax.ppermute(to_next, 'sky', swap(1))  3 us
    ppermute x1, waiting for transfers between devices, local(): from_next = lax.ppermute(to_next, 'sky', swap(1))  2.9 us
    ppermute x1, starting transfers between devices, local(): from_chip = lax.ppermute(to_chip, 'sky', swap(0))  1.6 us
    pallas_call x1, Pallas kernels, sum_call(): pl.pallas_call(sum_kernel, out_shape=(image, image, rows, rows), in_specs...  1.58 us
  transfers between devices with their start and end apart: 3, of which 2 were waited for; matrix products, arithmetic and copies ran while one was open for 0% of the time, Pallas kernels for 0%

profile of v7, /device:TPU:1, one launch (start us, length us, event | category | flops | bytes accessed | tf_op | source)
XLA Modules:
  0.0 56.9 jit_solution(15650567785063179455)
XLA Ops:
  1.3 5.2 %shard_map.122 = bf16[32,152,128]{2,1,0:T(8,128)(2,1)} custom-call(f32[3,1,5]{2,1,0:T(1,128)} %bitcast.4, bf16[1,1]{1,0:T(2,128)(2,1)} %bitcast.3.weight_hbm, s32[1,16]{1,0:T(1,128)} %bitcast.5, s32[1,16]{1,0:T(1,128)} %block_hbm.1, bf16[1,64,2048]{2,1,0:T(8,128)(2,1)} %tile_hbm.1, bf16[5,41]{1,0:T(8,128)(2,1)} %row_taps_hbm.1, bf16[5,41]{1,0:T(8,128)(2,1)} %col_taps_hbm.1, ...), custom_call_target="tpu_custom_call" | custom-call | tf_op jit(solution)/shard_map/pallas_call | solution.py:309
  6.5 12.6 %all-to-all-start = ((bf16[32,152,128]{2,1,0:T(8,128)(2,1)}), bf16[32,152,128]{2,1,0:T(8,128)(2,1)S(1)}, u32[]{:S(2)}, u32[]{:S(2)}) async-start(bf16[32,152,128]{2,1,0:T(8,128)(2,1)} %shard_map.122), calls=%async_computation | async-start | bytes 2490368 | tf_op jit(solution)/shard_map/all_to_all | solution.py:367
  19.1 0.2 shard_map.123
  19.2 27.5 %all-to-all-done.in_ref = bf16[32,152,128]{2,1,0:T(8,128)(2,1)S(1)} async-done(((bf16[32,152,128]{2,1,0:T(8,128)(2,1)}), bf16[32,152,128]{2,1,0:T(8,128)(2,1)S(1)}, u32[]{:S(2)}, u32[]{:S(2)}) %all-to-all-start) | async-done | bytes 1245216 | tf_op jit(solution)/shard_map/all_to_all | solution.py:367
  46.7 1.6 %shard_map.124 = (f32[64,2048]{1,0:T(8,128)}, f32[64,2048]{1,0:T(8,128)S(1)}, bf16[24,2048]{1,0:T(8,128)(2,1)S(1)}, bf16[24,2048]{1,0:T(8,128)(2,1)S(1)}) custom-call(bf16[32,152,128]{2,1,0:T(8,128)(2,1)S(1)} %all-to-all-done.in_ref, bf16[256,256]{1,0:T(8,128)(2,1)S(1)} %get-tuple-element.8.band_ref), custom_call_target="tpu_custom_call" | custom-call | tf_op jit(solution)/shard_map/pallas_call | solution.py:330
  48.3 1.6 %collective-permute-start = (bf16[24,2048]{1,0:T(8,128)(2,1)S(1)}, bf16[24,2048]{1,0:T(8,128)(2,1)S(1)}, u32[]{:S(2)}, u32[]{:S(2)}) collective-permute-start(bf16[24,2048]{1,0:T(8,128)(2,1)S(1)} %get-tuple-element.11), channel_id=1, source_target_pairs={{0,1},{1,0},{2,3},{3,2},{4,5},{5,4},{6,7},{7,6},{8,9},{9,8},{10,11... | collective-permute-start | bytes 294920 | tf_op jit(solution)/shard_map/ppermute | solution.py:372
  49.9 3.0 %collective-permute-start.1 = (bf16[24,2048]{1,0:T(8,128)(2,1)S(1)}, bf16[24,2048]{1,0:T(8,128)(2,1)S(1)}, u32[]{:S(2)}, u32[]{:S(2)}) collective-permute-start(bf16[24,2048]{1,0:T(8,128)(2,1)S(1)} %get-tuple-element.12), channel_id=1, source_target_pairs={{1,2},{2,1},{3,4},{4,3},{5,6},{6,5},{9,10},{10,9},{11,12},{12,11},... | collective-permute-start | bytes 294920 | tf_op jit(solution)/shard_map/ppermute | solution.py:371
  52.9 0.0 collective-permute-done.chip_ref
  52.9 2.9 %collective-permute-done.1.next_ref = bf16[24,2048]{1,0:T(8,128)(2,1)S(1)} collective-permute-done((bf16[24,2048]{1,0:T(8,128)(2,1)S(1)}, bf16[24,2048]{1,0:T(8,128)(2,1)S(1)}, u32[]{:S(2)}, u32[]{:S(2)}) %collective-permute-start.1) | collective-permute-done | bytes 98336 | tf_op jit(solution)/shard_map/ppermute | solution.py:371
  55.8 1.1 %shard_map.125 = f32[64,2048]{1,0:T(8,128)} custom-call(f32[64,2048]{1,0:T(8,128)S(1)} %get-tuple-element.10.mid_ref, bf16[24,2048]{1,0:T(8,128)(2,1)S(1)} %collective-permute-done.chip_ref, bf16[24,2048]{1,0:T(8,128)(2,1)S(1)} %collective-permute-done.1.next_ref, bf16[128,128]{1,0:T(8,128)(2,1)S(1)} %get-tuple-element.13.band_ref), custom_call_target="tpu_custom_call" | custom-call | tf_op jit(solution)/shard_map/pallas_call | solution.py:341
Async XLA Ops:
  6.5 40.2 %all-to-all-start = ((bf16[32,152,128]{2,1,0:T(8,128)(2,1)}), bf16[32,152,128]{2,1,0:T(8,128)(2,1)S(1)}, u32[]{:S(2)}, u32[]{:S(2)}) async-start(bf16[32,152,128]{2,1,0:T(8,128)(2,1)} %shard_map.122), calls=%async_computation | async-start | bytes 2490368 | tf_op jit(solution)/shard_map/all_to_all | solution.py:367
  48.3 4.6 %collective-permute-start = (bf16[24,2048]{1,0:T(8,128)(2,1)S(1)}, bf16[24,2048]{1,0:T(8,128)(2,1)S(1)}, u32[]{:S(2)}, u32[]{:S(2)}) collective-permute-start(bf16[24,2048]{1,0:T(8,128)(2,1)S(1)} %get-tuple-element.11), channel_id=1, source_target_pairs={{0,1},{1,0},{2,3},{3,2},{4,5},{5,4},{6,7},{7,6},{8,9},{9,8},{10,11... | collective-permute-start | bytes 294920 | tf_op jit(solution)/shard_map/ppermute | solution.py:372
  49.9 5.9 %collective-permute-start.1 = (bf16[24,2048]{1,0:T(8,128)(2,1)S(1)}, bf16[24,2048]{1,0:T(8,128)(2,1)S(1)}, u32[]{:S(2)}, u32[]{:S(2)}) collective-permute-start(bf16[24,2048]{1,0:T(8,128)(2,1)S(1)} %get-tuple-element.12), channel_id=1, source_target_pairs={{1,2},{2,1},{3,4},{4,3},{5,6},{6,5},{9,10},{10,9},{11,12},{12,11},... | collective-permute-start | bytes 294920 | tf_op jit(solution)/shard_map/ppermute | solution.py:371

commit v8 on v7

--- a/solution.py
+++ b/solution.py
@@ -99,6 +99,7 @@
     taps_ref[8:8 + NB, 0:KW] = col_taps_ref[...].astype(F32)
     row_band = jnp.concatenate([toeplitz(taps_ref[k:k + 1, :], LANES, 0) for k in range(NB)], axis=0).astype(BF)
     col_bands = [toeplitz(taps_ref[8 + k:9 + k, 0:LANES], R)[:, 0:R].astype(BF) for k in range(NB)]
+    empty = jnp.zeros((R, R), BF)
     moved = roll(tile_ref[0].astype(F32), HALO)
     before = iota((R, LANES), 1) < HALO
     for s in range(SPT + 1):
@@ -119,14 +120,25 @@
         column = iota((1, width), 1) + g * width
         x_coord = (2 * column - (W - 1)).astype(F32) / (W - 1)
         y_coord = (2 * iota((R, 1), 0) - (R - 1)).astype(F32) / (R - 1)
+        terms = [
+            jnp.concatenate(
+                [across[j * R:(j + 1) * R, k * LANES:(k + 1) * LANES] for j in range(group)], axis=1
+            )
+            for k in range(NB)
+        ]
+        basis_terms = []
+        for first in range(0, NB, 4):
+            count = min(4, NB - first)
+            bands = [
+                jnp.concatenate([col_bands[first + k] if k == j else empty for j in range(count)], axis=1)
+                for k in range(count)
+            ]
+            found = dot(jnp.concatenate(bands, axis=0), jnp.concatenate(terms[first:first + count], axis=0))
+            basis_terms += [found[k * R:(k + 1) * R] for k in range(count)]
         matched = jnp.zeros((R, width), F32)
         for k in range(NB):
-            term = jnp.concatenate(
-                [across[j * R:(j + 1) * R, k * LANES:(k + 1) * LANES] for j in range(group)], axis=1
-            )
-            basis_term = dot(col_bands[k], term)
             coeff_map = coeff_ref[0, 0, k] + coeff_ref[1, 0, k] * x_coord + coeff_ref[2, 0, k] * y_coord
-            matched = matched + coeff_map * basis_term
+            matched = matched + coeff_map * basis_terms[k]
         matched_ref[:, g * width:(g + 1) * width] = matched.astype(BF).astype(F32)
     for n in range(WINDOWS):
         first = n * SPAN - 2
@@ -215,12 +227,14 @@
     return jnp.concatenate([high, low], axis=0)
 
 
-def band_kernel(across_ref, down_ref):
+def band_kernel(across_ref, own_ref, halo_ref):
     across_ref[...] = taper_bands(2 * LANES, LANES, 0)
-    down_ref[...] = taper_bands(LANES, R, EDGE - HALO)
-
-
-def sum_kernel(in_ref, band_ref, coadd_ref, mid_ref, chip_ref, next_ref, stack_ref):
+    own_ref[...] = taper_bands(LANES, R, LANES - HALO)
+    band = taper_bands(LANES, R, EDGE - HALO).astype(F32)
+    halo_ref[...] = jnp.where(iota(band.shape, 1) < EDGE, band, roll(band, -R)).astype(BF)
+
+
+def sum_kernel(in_ref, band_ref, coadd_hbm, mid_ref, chip_ref, next_ref, stack_ref, coadd_ref, sem):
     peers = in_ref.shape[0]
     depth = peers * NOTE_LANES
     aux = [in_ref[v, NOTE:MSG, :].astype(F32) for v in range(peers)]
@@ -255,6 +269,8 @@
             value = total[rows, g * LANES:(g + 1) * LANES] * scale[rows]
             coadd_ref[g * UNIT:(g + 1) * UNIT, b * LANES:(b + 1) * LANES] = value
             stack_ref[(b + 1) * R + g * UNIT:(b + 1) * R + (g + 1) * UNIT, :] = value
+    copy = pltpu.make_async_copy(coadd_ref, coadd_hbm, sem)
+    copy.start()
     same = iota((AUX, depth), 0) == iota((AUX, depth), 1) % NOTE_LANES
     gap = jnp.zeros((NOTE_LANES - AUX, LANES), F32)
     edges = jnp.concatenate([x for v in range(peers) for x in (aux[v], gap)], axis=0).astype(BF)
@@ -282,18 +298,33 @@
     first, last = mid_ref[0:EDGE, :], mid_ref[R - EDGE:R, :]
     chip_ref[...] = jnp.where(even, last, first).astype(BF)
     next_ref[...] = jnp.where(even, first, last).astype(BF)
-
-
-def down_kernel(mid_ref, chip_ref, next_ref, band_ref, out_ref):
-    norm = sum((1.0 - (a / 21.0) ** 2) ** 2 for a in range(-HALO, HALO + 1))
+    copy.wait()
+
+
+SCALE = 1.0 / (441.0 * 441.0 * sum((1.0 - (a / 21.0) ** 2) ** 2 for a in range(-HALO, HALO + 1)))
+
+
+def own_kernel(mid_ref, band_ref, out_ref):
+    band = band_ref[:, 0:R]
+    high, low = split(mid_ref[...])
+    total = dot(jnp.concatenate([band, band], axis=1), jnp.concatenate([high, low], axis=0))
+    out_ref[...] = (total[0:R] + total[R:]) * SCALE
+
+
+def halo_kernel(own_ref, chip_ref, next_ref, band_ref, out_hbm, out_ref, sems):
     even = lax.axis_index("sky") % 2 == 0
-    chip, following = chip_ref[...].astype(F32), next_ref[...].astype(F32)
-    above, below = jnp.where(even, following, chip), jnp.where(even, chip, following)
-    rows = jnp.concatenate([above, mid_ref[...], below], axis=0)
-    band = band_ref[:, 0:R + 2 * EDGE]
-    high, low = split(rows)
-    total = dot(jnp.concatenate([band, band], axis=1), jnp.concatenate([high, low], axis=0))
-    out_ref[...] = (total[0:R] + total[R:]) * (1.0 / (441.0 * 441.0 * norm))
+    copies = []
+    width = W // 4
+    for c in range(4):
+        cols = slice(c * width, (c + 1) * width)
+        chip, following = chip_ref[:, cols].astype(F32), next_ref[:, cols].astype(F32)
+        above, below = jnp.where(even, following, chip), jnp.where(even, chip, following)
+        total = dot(band_ref[:, 0:2 * EDGE], jnp.concatenate([above, below], axis=0).astype(BF))
+        out_ref[:, cols] = own_ref[:, cols] + (total[0:R] + total[R:]) * SCALE
+        copies.append(pltpu.make_async_copy(out_ref.at[:, cols], out_hbm.at[:, cols], sems.at[c]))
+        copies[-1].start()
+    for copy in copies:
+        copy.wait()
 
 
 def vmem(n):
@@ -331,20 +362,35 @@
         sum_kernel,
         out_shape=(image, image, rows, rows),
         in_specs=vmem(2),
-        out_specs=tuple(vmem(4)),
-        scratch_shapes=[pltpu.VMEM(((SPT + 2) * R, LANES), F32)],
+        out_specs=(pl.BlockSpec(memory_space=pltpu.HBM), *vmem(3)),
+        scratch_shapes=[
+            pltpu.VMEM(((SPT + 2) * R, LANES), F32),
+            pltpu.VMEM((R, W), F32),
+            pltpu.SemaphoreType.DMA,
+        ],
         compiler_params=PARAMS,
     )(received, band)
 
 
-def down_call(mid, from_chip, from_next, band):
+def own_call(mid, band):
     return pl.pallas_call(
-        down_kernel,
+        own_kernel,
+        out_shape=jax.ShapeDtypeStruct((R, W), F32),
+        in_specs=vmem(2),
+        out_specs=pl.BlockSpec(memory_space=pltpu.VMEM),
+        compiler_params=PARAMS,
+    )(mid, band)
+
+
+def halo_call(own, from_chip, from_next, band):
+    return pl.pallas_call(
+        halo_kernel,
         out_shape=jax.ShapeDtypeStruct((R, W), F32),
         in_specs=vmem(4),
-        out_specs=pl.BlockSpec(memory_space=pltpu.VMEM),
+        out_specs=pl.BlockSpec(memory_space=pltpu.HBM),
+        scratch_shapes=[pltpu.VMEM((R, W), F32), pltpu.SemaphoreType.DMA((4,))],
         compiler_params=PARAMS,
-    )(mid, from_chip, from_next, band)
+    )(own, from_chip, from_next, band)
 
 
 def local(
@@ -357,10 +403,14 @@
         ccd_tiles, row_taps, col_taps, warp_start_x, warp_frac_x, warp_start_y, warp_frac_y,
     )
     messages = tile_call(peers, *operands)
-    band_across, band_down = pl.pallas_call(
+    band_across, band_own, band_halo = pl.pallas_call(
         band_kernel,
-        out_shape=(jax.ShapeDtypeStruct((2 * LANES, 2 * LANES), BF), jax.ShapeDtypeStruct((2 * R, LANES), BF)),
-        out_specs=tuple(vmem(2)),
+        out_shape=(
+            jax.ShapeDtypeStruct((2 * LANES, 2 * LANES), BF),
+            jax.ShapeDtypeStruct((2 * R, LANES), BF),
+            jax.ShapeDtypeStruct((2 * R, LANES), BF),
+        ),
+        out_specs=tuple(vmem(3)),
         compiler_params=PARAMS,
     )()
     groups = [sorted(range(peers), key=seat)]
@@ -370,7 +420,7 @@
     swap = lambda first: [p for i in range(first, size - 1, 2) for p in ((i, i + 1), (i + 1, i))]
     from_next = lax.ppermute(to_next, "sky", swap(1))
     from_chip = lax.ppermute(to_chip, "sky", swap(0))
-    detection = down_call(mid, from_chip, from_next, band_down)
+    detection = halo_call(own_call(mid, band_own), from_chip, from_next, band_halo)
     return coadd, detection
 
 

time: 57.1 us -> 57 us (level)
    pallas_call x1 -> x2, Pallas kernels: 1.14 us -> 1.34 us  [the longest x1 1 us: halo_call(): pl.pallas_call(halo_kernel, out_shape=jax.ShapeDtypeStruct((R, W), F32),...]
  transfers between devices with their start and end apart: 3 -> 3, of which waited for: 2 -> 2; matrix products, arithmetic and copies ran while one was open for 0% -> 0% of each run, Pallas kernels for 0% -> 1%
where the time goes in v8:
time: 57 us; the launch traced here: 56.7 us
  waiting for transfers between devices  29.9 us (52%)
  starting transfers between devices  17.4 us (31%)
  Pallas kernels  8.13 us (14%)
  between operations  1.34 us (2%)
    all_to_all x1, waiting for transfers between devices, local(): lax.all_to_all(messages, 'visit', 0, 0, tiled=True, axis_index_groups=gro...  27.4 us
    all_to_all x1, starting transfers between devices, local(): lax.all_to_all(messages, 'visit', 0, 0, tiled=True, axis_index_groups=gro...  12.8 us
    pallas_call x1, Pallas kernels, tile_call(): pl.pallas_call(tile_kernel, out_shape=jax.ShapeDtypeStruct((peers, MSG, L...  4.97 us
    ppermute x1, starting transfers between devices, local(): from_next = lax.ppermute(to_next, 'sky', swap(1))  3.14 us
    ppermute x1, waiting for transfers between devices, local(): from_next = lax.ppermute(to_next, 'sky', swap(1))  2.42 us
    pallas_call x1, Pallas kernels, sum_call(): pl.pallas_call(sum_kernel, out_shape=(image, image, rows, rows), in_specs...  1.59 us
    ppermute x1, starting transfers between devices, local(): from_chip = lax.ppermute(to_chip, 'sky', swap(0))  1.48 us
  transfers between devices with their start and end apart: 3, of which 2 were waited for; matrix products, arithmetic and copies ran while one was open for 0% of the time, Pallas kernels for 1%

profile of v8, /device:TPU:1, one launch (start us, length us, event | category | flops | bytes accessed | tf_op | source)
XLA Modules:
  0.0 56.7 jit_solution(8386394809398264406)
XLA Ops:
  1.3 5.0 %shard_map.122 = bf16[32,152,128]{2,1,0:T(8,128)(2,1)} custom-call(f32[3,1,5]{2,1,0:T(1,128)} %bitcast.4, bf16[1,1]{1,0:T(2,128)(2,1)} %bitcast.3.weight_hbm, s32[1,16]{1,0:T(1,128)} %bitcast.5, s32[1,16]{1,0:T(1,128)} %block_hbm.1, bf16[1,64,2048]{2,1,0:T(8,128)(2,1)} %tile_hbm.1, bf16[5,41]{1,0:T(8,128)(2,1)} %row_taps_hbm.1, bf16[5,41]{1,0:T(8,128)(2,1)} %col_taps_hbm.1, ...), custom_call_target="tpu_custom_call" | custom-call | tf_op jit(solution)/shard_map/pallas_call | solution.py:340
  6.3 12.8 %all-to-all-start = ((bf16[32,152,128]{2,1,0:T(8,128)(2,1)}), bf16[32,152,128]{2,1,0:T(8,128)(2,1)S(1)}, u32[]{:S(2)}, u32[]{:S(2)}) async-start(bf16[32,152,128]{2,1,0:T(8,128)(2,1)} %shard_map.122), calls=%async_computation | async-start | bytes 2490368 | tf_op jit(solution)/shard_map/all_to_all | solution.py:417
  19.1 0.2 shard_map.123
  19.3 27.4 %all-to-all-done.in_ref = bf16[32,152,128]{2,1,0:T(8,128)(2,1)S(1)} async-done(((bf16[32,152,128]{2,1,0:T(8,128)(2,1)}), bf16[32,152,128]{2,1,0:T(8,128)(2,1)S(1)}, u32[]{:S(2)}, u32[]{:S(2)}) %all-to-all-start) | async-done | bytes 1245216 | tf_op jit(solution)/shard_map/all_to_all | solution.py:417
  46.7 1.6 %shard_map.124 = (f32[64,2048]{1,0:T(8,128)}, f32[64,2048]{1,0:T(8,128)S(1)}, bf16[24,2048]{1,0:T(8,128)(2,1)S(1)}, bf16[24,2048]{1,0:T(8,128)(2,1)S(1)}) custom-call(bf16[32,152,128]{2,1,0:T(8,128)(2,1)S(1)} %all-to-all-done.in_ref, bf16[256,256]{1,0:T(8,128)(2,1)S(1)} %get-tuple-element.9.band_ref), custom_call_target="tpu_custom_call" | custom-call | tf_op jit(solution)/shard_map/pallas_call | solution.py:361
  48.3 1.5 %collective-permute-start = (bf16[24,2048]{1,0:T(8,128)(2,1)S(1)}, bf16[24,2048]{1,0:T(8,128)(2,1)S(1)}, u32[]{:S(2)}, u32[]{:S(2)}) collective-permute-start(bf16[24,2048]{1,0:T(8,128)(2,1)S(1)} %get-tuple-element.13), channel_id=1, source_target_pairs={{0,1},{1,0},{2,3},{3,2},{4,5},{5,4},{6,7},{7,6},{8,9},{9,8},{10,11... | collective-permute-start | bytes 294920 | tf_op jit(solution)/shard_map/ppermute | solution.py:422
  49.8 3.1 %collective-permute-start.1 = (bf16[24,2048]{1,0:T(8,128)(2,1)S(1)}, bf16[24,2048]{1,0:T(8,128)(2,1)S(1)}, u32[]{:S(2)}, u32[]{:S(2)}) collective-permute-start(bf16[24,2048]{1,0:T(8,128)(2,1)S(1)} %get-tuple-element.14), channel_id=1, source_target_pairs={{1,2},{2,1},{3,4},{4,3},{5,6},{6,5},{9,10},{10,9},{11,12},{12,11},... | collective-permute-start | bytes 294920 | tf_op jit(solution)/shard_map/ppermute | solution.py:421
  52.9 0.3 shard_map.125.own_ref
  53.3 0.0 collective-permute-done.chip_ref
  53.3 2.4 %collective-permute-done.1.next_ref = bf16[24,2048]{1,0:T(8,128)(2,1)S(1)} collective-permute-done((bf16[24,2048]{1,0:T(8,128)(2,1)S(1)}, bf16[24,2048]{1,0:T(8,128)(2,1)S(1)}, u32[]{:S(2)}, u32[]{:S(2)}) %collective-permute-start.1) | collective-permute-done | bytes 98336 | tf_op jit(solution)/shard_map/ppermute | solution.py:421
  55.7 1.0 %shard_map.126 = f32[64,2048]{1,0:T(8,128)} custom-call(f32[64,2048]{1,0:T(8,128)S(1)} %shard_map.125.own_ref, bf16[24,2048]{1,0:T(8,128)(2,1)S(1)} %collective-permute-done.chip_ref, bf16[24,2048]{1,0:T(8,128)(2,1)S(1)} %collective-permute-done.1.next_ref, bf16[128,128]{1,0:T(8,128)(2,1)S(1)} %get-tuple-element.15.band_ref), custom_call_target="tpu_custom_call" | custom-call | tf_op jit(solution)/shard_map/pallas_call | solution.py:386
Async XLA Ops:
  6.3 40.4 %all-to-all-start = ((bf16[32,152,128]{2,1,0:T(8,128)(2,1)}), bf16[32,152,128]{2,1,0:T(8,128)(2,1)S(1)}, u32[]{:S(2)}, u32[]{:S(2)}) async-start(bf16[32,152,128]{2,1,0:T(8,128)(2,1)} %shard_map.122), calls=%async_computation | async-start | bytes 2490368 | tf_op jit(solution)/shard_map/all_to_all | solution.py:417
  48.3 5.0 %collective-permute-start = (bf16[24,2048]{1,0:T(8,128)(2,1)S(1)}, bf16[24,2048]{1,0:T(8,128)(2,1)S(1)}, u32[]{:S(2)}, u32[]{:S(2)}) collective-permute-start(bf16[24,2048]{1,0:T(8,128)(2,1)S(1)} %get-tuple-element.13), channel_id=1, source_target_pairs={{0,1},{1,0},{2,3},{3,2},{4,5},{5,4},{6,7},{7,6},{8,9},{9,8},{10,11... | collective-permute-start | bytes 294920 | tf_op jit(solution)/shard_map/ppermute | solution.py:422
  49.8 5.9 %collective-permute-start.1 = (bf16[24,2048]{1,0:T(8,128)(2,1)S(1)}, bf16[24,2048]{1,0:T(8,128)(2,1)S(1)}, u32[]{:S(2)}, u32[]{:S(2)}) collective-permute-start(bf16[24,2048]{1,0:T(8,128)(2,1)S(1)} %get-tuple-element.14), channel_id=1, source_target_pairs={{1,2},{2,1},{3,4},{4,3},{5,6},{6,5},{9,10},{10,9},{11,12},{12,11},... | collective-permute-start | bytes 294920 | tf_op jit(solution)/shard_map/ppermute | solution.py:421

commit v9 on v7

--- a/solution.py
+++ b/solution.py
@@ -99,6 +99,7 @@
     taps_ref[8:8 + NB, 0:KW] = col_taps_ref[...].astype(F32)
     row_band = jnp.concatenate([toeplitz(taps_ref[k:k + 1, :], LANES, 0) for k in range(NB)], axis=0).astype(BF)
     col_bands = [toeplitz(taps_ref[8 + k:9 + k, 0:LANES], R)[:, 0:R].astype(BF) for k in range(NB)]
+    empty = jnp.zeros((R, R), BF)
     moved = roll(tile_ref[0].astype(F32), HALO)
     before = iota((R, LANES), 1) < HALO
     for s in range(SPT + 1):
@@ -119,14 +120,25 @@
         column = iota((1, width), 1) + g * width
         x_coord = (2 * column - (W - 1)).astype(F32) / (W - 1)
         y_coord = (2 * iota((R, 1), 0) - (R - 1)).astype(F32) / (R - 1)
+        terms = [
+            jnp.concatenate(
+                [across[j * R:(j + 1) * R, k * LANES:(k + 1) * LANES] for j in range(group)], axis=1
+            )
+            for k in range(NB)
+        ]
+        basis_terms = []
+        for first in range(0, NB, 4):
+            count = min(4, NB - first)
+            bands = [
+                jnp.concatenate([col_bands[first + k] if k == j else empty for j in range(count)], axis=1)
+                for k in range(count)
+            ]
+            found = dot(jnp.concatenate(bands, axis=0), jnp.concatenate(terms[first:first + count], axis=0))
+            basis_terms += [found[k * R:(k + 1) * R] for k in range(count)]
         matched = jnp.zeros((R, width), F32)
         for k in range(NB):
-            term = jnp.concatenate(
-                [across[j * R:(j + 1) * R, k * LANES:(k + 1) * LANES] for j in range(group)], axis=1
-            )
-            basis_term = dot(col_bands[k], term)
             coeff_map = coeff_ref[0, 0, k] + coeff_ref[1, 0, k] * x_coord + coeff_ref[2, 0, k] * y_coord
-            matched = matched + coeff_map * basis_term
+            matched = matched + coeff_map * basis_terms[k]
         matched_ref[:, g * width:(g + 1) * width] = matched.astype(BF).astype(F32)
     for n in range(WINDOWS):
         first = n * SPAN - 2

time: 57.1 us -> 57 us (level)
  no operation moved by 1% of the time
where the time goes in v9:
time: 57 us; the launch traced here: 56.8 us
  waiting for transfers between devices  30.3 us (53%)
  starting transfers between devices  17.1 us (30%)
  Pallas kernels  7.98 us (14%)
  between operations  1.32 us (2%)
    all_to_all x1, waiting for transfers between devices, local(): lax.all_to_all(messages, 'visit', 0, 0, tiled=True, axis_index_groups=gro...  27.5 us
    all_to_all x1, starting transfers between devices, local(): lax.all_to_all(messages, 'visit', 0, 0, tiled=True, axis_index_groups=gro...  12.6 us
    pallas_call x1, Pallas kernels, tile_call(): pl.pallas_call(tile_kernel, out_shape=jax.ShapeDtypeStruct((peers, MSG, L...  5.1 us
    ppermute x1, starting transfers between devices, local(): from_next = lax.ppermute(to_next, 'sky', swap(1))  3.04 us
    ppermute x1, waiting for transfers between devices, local(): from_next = lax.ppermute(to_next, 'sky', swap(1))  2.87 us
    pallas_call x1, Pallas kernels, sum_call(): pl.pallas_call(sum_kernel, out_shape=(image, image, rows, rows), in_specs...  1.58 us
    ppermute x1, starting transfers between devices, local(): from_chip = lax.ppermute(to_chip, 'sky', swap(0))  1.52 us
  transfers between devices with their start and end apart: 3, of which 2 were waited for; matrix products, arithmetic and copies ran while one was open for 0% of the time, Pallas kernels for 0%

profile of v9, /device:TPU:1, one launch (start us, length us, event | category | flops | bytes accessed | tf_op | source)
XLA Modules:
  0.0 56.8 jit_solution(2176538349500048860)
XLA Ops:
  1.3 5.1 %shard_map.122 = bf16[32,152,128]{2,1,0:T(8,128)(2,1)} custom-call(f32[3,1,5]{2,1,0:T(1,128)} %bitcast.4, bf16[1,1]{1,0:T(2,128)(2,1)} %bitcast.3.weight_hbm, s32[1,16]{1,0:T(1,128)} %bitcast.5, s32[1,16]{1,0:T(1,128)} %block_hbm.1, bf16[1,64,2048]{2,1,0:T(8,128)(2,1)} %tile_hbm.1, bf16[5,41]{1,0:T(8,128)(2,1)} %row_taps_hbm.1, bf16[5,41]{1,0:T(8,128)(2,1)} %col_taps_hbm.1, ...), custom_call_target="tpu_custom_call" | custom-call | tf_op jit(solution)/shard_map/pallas_call | solution.py:321
  6.4 12.6 %all-to-all-start = ((bf16[32,152,128]{2,1,0:T(8,128)(2,1)}), bf16[32,152,128]{2,1,0:T(8,128)(2,1)S(1)}, u32[]{:S(2)}, u32[]{:S(2)}) async-start(bf16[32,152,128]{2,1,0:T(8,128)(2,1)} %shard_map.122), calls=%async_computation | async-start | bytes 2490368 | tf_op jit(solution)/shard_map/all_to_all | solution.py:379
  19.0 0.2 shard_map.123
  19.1 27.5 %all-to-all-done.in_ref = bf16[32,152,128]{2,1,0:T(8,128)(2,1)S(1)} async-done(((bf16[32,152,128]{2,1,0:T(8,128)(2,1)}), bf16[32,152,128]{2,1,0:T(8,128)(2,1)S(1)}, u32[]{:S(2)}, u32[]{:S(2)}) %all-to-all-start) | async-done | bytes 1245216 | tf_op jit(solution)/shard_map/all_to_all | solution.py:379
  46.6 1.6 %shard_map.124 = (f32[64,2048]{1,0:T(8,128)}, f32[64,2048]{1,0:T(8,128)S(1)}, bf16[24,2048]{1,0:T(8,128)(2,1)S(1)}, bf16[24,2048]{1,0:T(8,128)(2,1)S(1)}) custom-call(bf16[32,152,128]{2,1,0:T(8,128)(2,1)S(1)} %all-to-all-done.in_ref, bf16[256,256]{1,0:T(8,128)(2,1)S(1)} %get-tuple-element.8.band_ref), custom_call_target="tpu_custom_call" | custom-call | tf_op jit(solution)/shard_map/pallas_call | solution.py:342
  48.2 1.5 %collective-permute-start = (bf16[24,2048]{1,0:T(8,128)(2,1)S(1)}, bf16[24,2048]{1,0:T(8,128)(2,1)S(1)}, u32[]{:S(2)}, u32[]{:S(2)}) collective-permute-start(bf16[24,2048]{1,0:T(8,128)(2,1)S(1)} %get-tuple-element.11), channel_id=1, source_target_pairs={{0,1},{1,0},{2,3},{3,2},{4,5},{5,4},{6,7},{7,6},{8,9},{9,8},{10,11... | collective-permute-start | bytes 294920 | tf_op jit(solution)/shard_map/ppermute | solution.py:384
  49.7 3.0 %collective-permute-start.1 = (bf16[24,2048]{1,0:T(8,128)(2,1)S(1)}, bf16[24,2048]{1,0:T(8,128)(2,1)S(1)}, u32[]{:S(2)}, u32[]{:S(2)}) collective-permute-start(bf16[24,2048]{1,0:T(8,128)(2,1)S(1)} %get-tuple-element.12), channel_id=1, source_target_pairs={{1,2},{2,1},{3,4},{4,3},{5,6},{6,5},{9,10},{10,9},{11,12},{12,11},... | collective-permute-start | bytes 294920 | tf_op jit(solution)/shard_map/ppermute | solution.py:383
  52.8 0.0 collective-permute-done.chip_ref
  52.8 2.9 %collective-permute-done.1.next_ref = bf16[24,2048]{1,0:T(8,128)(2,1)S(1)} collective-permute-done((bf16[24,2048]{1,0:T(8,128)(2,1)S(1)}, bf16[24,2048]{1,0:T(8,128)(2,1)S(1)}, u32[]{:S(2)}, u32[]{:S(2)}) %collective-permute-start.1) | collective-permute-done | bytes 98336 | tf_op jit(solution)/shard_map/ppermute | solution.py:383
  55.6 1.1 %shard_map.125 = f32[64,2048]{1,0:T(8,128)} custom-call(f32[64,2048]{1,0:T(8,128)S(1)} %get-tuple-element.10.mid_ref, bf16[24,2048]{1,0:T(8,128)(2,1)S(1)} %collective-permute-done.chip_ref, bf16[24,2048]{1,0:T(8,128)(2,1)S(1)} %collective-permute-done.1.next_ref, bf16[128,128]{1,0:T(8,128)(2,1)S(1)} %get-tuple-element.13.band_ref), custom_call_target="tpu_custom_call" | custom-call | tf_op jit(solution)/shard_map/pallas_call | solution.py:353
Async XLA Ops:
  6.4 40.2 %all-to-all-start = ((bf16[32,152,128]{2,1,0:T(8,128)(2,1)}), bf16[32,152,128]{2,1,0:T(8,128)(2,1)S(1)}, u32[]{:S(2)}, u32[]{:S(2)}) async-start(bf16[32,152,128]{2,1,0:T(8,128)(2,1)} %shard_map.122), calls=%async_computation | async-start | bytes 2490368 | tf_op jit(solution)/shard_map/all_to_all | solution.py:379
  48.2 4.6 %collective-permute-start = (bf16[24,2048]{1,0:T(8,128)(2,1)S(1)}, bf16[24,2048]{1,0:T(8,128)(2,1)S(1)}, u32[]{:S(2)}, u32[]{:S(2)}) collective-permute-start(bf16[24,2048]{1,0:T(8,128)(2,1)S(1)} %get-tuple-element.11), channel_id=1, source_target_pairs={{0,1},{1,0},{2,3},{3,2},{4,5},{5,4},{6,7},{7,6},{8,9},{9,8},{10,11... | collective-permute-start | bytes 294920 | tf_op jit(solution)/shard_map/ppermute | solution.py:384
  49.7 5.9 %collective-permute-start.1 = (bf16[24,2048]{1,0:T(8,128)(2,1)S(1)}, bf16[24,2048]{1,0:T(8,128)(2,1)S(1)}, u32[]{:S(2)}, u32[]{:S(2)}) collective-permute-start(bf16[24,2048]{1,0:T(8,128)(2,1)S(1)} %get-tuple-element.12), channel_id=1, source_target_pairs={{1,2},{2,1},{3,4},{4,3},{5,6},{6,5},{9,10},{10,9},{11,12},{12,11},... | collective-permute-start | bytes 294920 | tf_op jit(solution)/shard_map/ppermute | solution.py:383
